TPU v7x, 32 devices: a whole 2x2x4 slice. The times are simulated.
32 devices in a mesh: half: 2 (over x), quarter: 2 (over y), grp: 8 (over z, core).
Axes of the slice: x: 2, y: 2, z: 4, core: 2. Of those that a mesh axis runs over, the one named last changes fastest.
Arguments:
- rhs: float32 [8192, 512], P(('half', 'quarter', 'grp')), may hold values from -6 to 6
- left_one: float32 [8192, 128], P(('half', 'quarter', 'grp')), may hold values from -0.5 to 0.5
- left_two: float32 [8192, 128], P(('half', 'quarter', 'grp')), may hold values from -0.5 to 0.5
- middle_one: float32 [2, 8, 128, 128], P('half', 'grp'), may hold values from -0.5 to 0.5
- middle_two: float32 [4, 8, 128, 128], P(('half', 'quarter'), 'grp'), may hold values from -0.5 to 0.5
- right_one: float32 [8192, 128], P(('half', 'quarter', 'grp')), may hold values from -0.25 to 0.25
- right_two: float32 [8192, 128], P(('half', 'quarter', 'grp')), may hold values from -0.375 to 0.375
- order_one: int32 [2, 8, 8], P('half', 'grp'), may hold values from 0 to 7, each once within a row
- order_two: int32 [4, 8, 8], P(('half', 'quarter'), 'grp'), may hold values from 0 to 7, each once within a row
Outputs:
- product: float32 [8192, 512], P(('half', 'quarter', 'grp'))
Inputs may be any that keep to these rules, and one draw needn't show every extreme that they name: `order_one`: each row along the last dimension is a permutation of 0 .. 7. `order_two`: each row along the last dimension is a permutation of 0 .. 7.
All inputs are finite; a program needn't handle non-finite values.
Results may differ from a plain program's by a relative error of at most 0.000071.
Values sent between devices are 32-bit elements; how exact they have to be, the bound alone decides.
No kernel may reach another device: no remote copies, remote signals or barrier semaphores. Data moves between devices by JAX's collectives and lax.ppermute only.
A program may use at most 64 MiB of HBM per device.

v0:
```python
import jax
import jax.numpy as jnp
from jax import lax
from jax.sharding import PartitionSpec as P


def swapped(value, axis, distance):
    mask = 2**distance
    pairs = [(source, source ^ mask) for source in range(lax.axis_size(axis))]
    return lax.ppermute(value, axis, pairs)


def matmul(left, right):
    return jnp.dot(left, right, precision=lax.Precision.HIGHEST, preferred_element_type=jnp.float32)


def project(factor, values):
    return lax.dot_general(
        factor,
        values,
        (((0,), (0,)), ((), ())),
        precision=lax.Precision.HIGHEST,
        preferred_element_type=jnp.float32,
    )


def to_slots(coeffs, order):
    groups = order.shape[0]
    parts = coeffs.reshape(groups, coeffs.shape[0] // groups, coeffs.shape[1])
    return jnp.take(parts, jnp.argsort(order), axis=0)


def on_device(
    rhs, left_one, left_two, middle_one, middle_two, right_one, right_two, order_one, order_two
):
    coeff_two = project(right_two, rhs)
    slots_two = to_slots(coeff_two, order_two[0, 0])
    partial_value = project(right_one, rhs)
    reduced = lax.psum(partial_value, "quarter")
    slots_one = to_slots(reduced, order_one[0, 0])
    received = lax.all_to_all(slots_two, "grp", split_axis=0, concat_axis=0, tiled=True)
    stacked = received.reshape(-1, received.shape[2])
    sibling = swapped(stacked, "quarter", 0)
    result_two = matmul(left_two, matmul(middle_two[0, 0], sibling))
    received = lax.all_to_all(slots_one, "grp", split_axis=0, concat_axis=0, tiled=True)
    stacked = received.reshape(-1, received.shape[2])
    sibling = swapped(stacked, "half", 0)
    result_one = matmul(left_one, matmul(middle_one[0, 0], sibling))
    return result_one + result_two


def solution(mesh):
    in_specs = (
        P(("half", "quarter", "grp"), None),
        P(("half", "quarter", "grp"), None),
        P(("half", "quarter", "grp"), None),
        P("half", "grp", None, None),
        P(("half", "quarter"), "grp", None, None),
        P(("half", "quarter", "grp"), None),
        P(("half", "quarter", "grp"), None),
        P("half", "grp", None),
        P(("half", "quarter"), "grp", None),
    )
    out_specs = P(("half", "quarter", "grp"), None)
    return jax.shard_map(
        on_device, mesh=mesh, in_specs=in_specs, out_specs=out_specs, check_vma=False
    )
```

profile of v0, /device:TPU:0, one launch (start us, length us, event | category | flops | bytes accessed | tf_op | source)
XLA Modules:
  0.0 70.2 jit_solution(7340464429655674874)
XLA Ops:
  6.5 0.0 copy-start
  6.5 0.0 all-reduce.2.cloned.1.call-start
  6.5 1.0 %copy-done = f32[256,512]{1,0:T(8,128)S(1)} copy-done((f32[256,512]{1,0:T(8,128)S(1)}, f32[256,512]{1,0:T(8,128)}, u32[]{:S(2)}) %copy-start) | copy-done | bytes 524312
  7.6 2.1 %fusion.5 = f32[128,512]{1,0:T(8,128)} fusion(f32[256,128]{1,0:T(8,128)} %param.16, f32[256,512]{1,0:T(8,128)S(1)} %copy-done), kind=kOutput, calls=%fused_computation.16 | convolution fusion | flops 201326592 | bytes 917504 | tf_op jit(solution)/shard_map/dot_general | solution.py:18
  9.6 0.0 copy-start.1
  9.6 0.0 all-reduce.2.cloned.1.call-update
  9.7 0.0 copy-start.6
  9.7 0.7 copy-done.6
  10.4 1.0 %sort.32 = (s32[8]{0:T(128)}, s32[8]{0:T(128)S(1)}) sort(s32[8]{0:T(128)S(1)} %bitcast.28, s32[8]{0:T(128)S(1)} %iota.8), dimensions={0}, to_apply=%region_2.4 | sort | flops 24 | bytes 128 | tf_op jit(solution)/shard_map/jit(argsort)/sort | solution.py:30
  11.4 0.0 copy-done.1
  11.4 0.5 fusion.7
  11.9 0.6 gather_fusion.1
  12.4 0.8 %broadcast_select_fusion = f32[8,16,512]{2,1,0:T(8,128)} fusion(f32[8,16,512]{2,1,0:T(8,128)S(1)} %gather_fusion.1, pred[8]{0:T(512)(128)(4,1)S(1)} %compare_and_fusion), kind=kLoop, calls=%fused_computation.4 | loop fusion | flops 65536 | bytes 524296 | tf_op jit(solution)/shard_map/jit(_take)/select_n | solution.py:30
  13.2 6.3 %all-to-all-start.1 = ((f32[8,16,512]{2,1,0:T(8,128)}), f32[8,16,512]{2,1,0:T(8,128)S(1)}, u32[]{:S(2)}, u32[]{:S(2)}) async-start(f32[8,16,512]{2,1,0:T(8,128)} %broadcast_select_fusion), calls=%async_computation.1 | async-start | bytes 524288 | tf_op jit(solution)/shard_map/all_to_all | solution.py:41
  19.6 0.0 copy-start.7
  19.6 0.6 copy-done.7
  20.2 1.0 %sort.31 = (s32[8]{0:T(128)}, s32[8]{0:T(128)S(1)}) sort(s32[8]{0:T(128)S(1)} %bitcast.29, s32[8]{0:T(128)S(1)} %iota.7), dimensions={0}, to_apply=%region_1.2 | sort | flops 24 | bytes 128 | tf_op jit(solution)/shard_map/jit(argsort)/sort | solution.py:30
  21.3 14.4 %all-reduce.2.cloned.1.call-done = f32[8,16,512]{2,1,0:T(8,128)} async-done(((f32[8,16,512]{2,1,0:T(8,128)}), f32[8,16,512]{2,1,0:T(8,128)}) %all-reduce.2.cloned.1.call-update) | async-done | bytes 262160 | tf_op jit(solution)/shard_map/psum | solution.py:39
  35.7 1.5 %gather_fusion = f32[8,16,512]{2,1,0:T(8,128)S(1)} fusion(f32[8,16,512]{2,1,0:T(8,128)} %all-reduce.2.cloned.1.call-done, s32[1024]{0:T(1024)S(1)} %pad_clamp_fusion.1), kind=kCustom, calls=%fused_computation.clone | custom fusion | bytes 524320 | tf_op jit(solution)/shard_map/jit(_take)/gather | solution.py:30
  37.2 0.8 %broadcast_select_fusion.1 = f32[8,16,512]{2,1,0:T(8,128)} fusion(f32[8,16,512]{2,1,0:T(8,128)S(1)} %gather_fusion, pred[8]{0:T(512)(128)(4,1)S(1)} %compare_and_fusion.1), kind=kLoop, calls=%fused_computation.5 | loop fusion | flops 65536 | bytes 524296 | tf_op jit(solution)/shard_map/jit(_take)/select_n | solution.py:30
  38.0 0.0 copy-start.4
  38.0 0.0 all-to-all-done.1
  38.0 4.7 %all-to-all-start = ((f32[8,16,512]{2,1,0:T(8,128)}), f32[8,16,512]{2,1,0:T(8,128)S(1)}, u32[]{:S(2)}, u32[]{:S(2)}) async-start(f32[8,16,512]{2,1,0:T(8,128)} %broadcast_select_fusion.1), calls=%async_computation | async-start | bytes 524288 | tf_op jit(solution)/shard_map/all_to_all | solution.py:45
  42.8 0.6 collective-permute-start.1
  43.3 9.2 %all-to-all-done = f32[8,16,512]{2,1,0:T(8,128)S(1)} async-done(((f32[8,16,512]{2,1,0:T(8,128)}), f32[8,16,512]{2,1,0:T(8,128)S(1)}, u32[]{:S(2)}, u32[]{:S(2)}) %all-to-all-start) | async-done | bytes 262176 | tf_op jit(solution)/shard_map/all_to_all | solution.py:45
  52.5 0.0 copy-start.5
  52.5 1.5 %collective-permute-start = (f32[128,512]{1,0:T(8,128)S(1)}, f32[128,512]{1,0:T(8,128)S(1)}, u32[]{:S(2)}, u32[]{:S(2)}) collective-permute-start(f32[128,512]{1,0:T(8,128)S(1)} %bitcast.27), channel_id=1, source_target_pairs={{0,16},{16,0},{1,17},{17,1},{2,18},{18,2},{3,19},{19,3},{4,20},{20... | collective-permute-start | bytes 786440 | tf_op jit(solution)/shard_map/ppermute | solution.py:10
  54.0 0.0 collective-permute-done.1
  54.0 0.0 copy-done.4
  54.0 0.6 fusion.1
  54.6 0.0 copy-start.2
  54.6 5.6 %collective-permute-done = f32[128,512]{1,0:T(8,128)S(1)} collective-permute-done((f32[128,512]{1,0:T(8,128)S(1)}, f32[128,512]{1,0:T(8,128)S(1)}, u32[]{:S(2)}, u32[]{:S(2)}) %collective-permute-start) | collective-permute-done | bytes 262176 | tf_op jit(solution)/shard_map/ppermute | solution.py:10
  60.2 0.0 copy-done.5
  60.2 0.6 fusion.3
  60.8 0.0 copy-done.2
  60.8 0.0 copy-start.3
  60.8 0.6 fusion.6
  61.4 0.3 copy-done.3
  61.7 0.6 fusion
  62.3 1.0 %copy.10 = f32[256,512]{1,0:T(8,128)} copy(f32[256,512]{0,1:T(8,128)S(1)} %fusion) | data formatting | bytes 1048576 | tf_op jit(solution)/shard_map/add | solution.py:49
  (8 shorter events, 0.0 us)
Async XLA Ops:
  6.5 1.0 %copy-start = (f32[256,512]{1,0:T(8,128)S(1)}, f32[256,512]{1,0:T(8,128)}, u32[]{:S(2)}) copy-start(f32[256,512]{1,0:T(8,128)} %param.11) | copy-start | bytes 1572868
  6.5 29.2 %all-reduce.2.cloned.1.call-start = ((), (), s32[]{:S(2)}) async-start(), calls=%async_computation.2 | async-start | bytes 524288 | tf_op jit(solution)/shard_map/psum | solution.py:39
  9.6 1.8 %copy-start.1 = (f32[256,128]{1,0:T(8,128)S(1)}, f32[256,128]{1,0:T(8,128)}, u32[]{:S(2)}) copy-start(f32[256,128]{1,0:T(8,128)} %param.17) | copy-start | bytes 393220
  9.7 0.7 copy-start.6
  13.2 24.8 %all-to-all-start.1 = ((f32[8,16,512]{2,1,0:T(8,128)}), f32[8,16,512]{2,1,0:T(8,128)S(1)}, u32[]{:S(2)}, u32[]{:S(2)}) async-start(f32[8,16,512]{2,1,0:T(8,128)} %broadcast_select_fusion), calls=%async_computation.1 | async-start | bytes 524288 | tf_op jit(solution)/shard_map/all_to_all | solution.py:41
  19.6 0.7 copy-start.7
  38.0 16.0 %copy-start.4 = (f32[1,1,128,128]{3,2,1,0:T(8,128)S(1)}, f32[1,1,128,128]{3,2,1,0:T(8,128)}, u32[]{:S(2)}) copy-start(f32[1,1,128,128]{3,2,1,0:T(8,128)} %param.15) | copy-start | bytes 196612
  38.0 14.5 %all-to-all-start = ((f32[8,16,512]{2,1,0:T(8,128)}), f32[8,16,512]{2,1,0:T(8,128)S(1)}, u32[]{:S(2)}, u32[]{:S(2)}) async-start(f32[8,16,512]{2,1,0:T(8,128)} %broadcast_select_fusion.1), calls=%async_computation | async-start | bytes 524288 | tf_op jit(solution)/shard_map/all_to_all | solution.py:45
  42.8 11.2 %collective-permute-start.1 = (f32[128,512]{1,0:T(8,128)S(1)}, f32[128,512]{1,0:T(8,128)S(1)}, u32[]{:S(2)}, u32[]{:S(2)}) collective-permute-start(f32[128,512]{1,0:T(8,128)S(1)} %bitcast.26), channel_id=1, source_target_pairs={{0,8},{8,0},{1,9},{9,1},{2,10},{10,2},{3,11},{11,3},{4,12},{12,4},... | collective-permute-start | bytes 786440 | tf_op jit(solution)/shard_map/ppermute | solution.py:10
  52.5 7.7 %copy-start.5 = (f32[1,1,128,128]{3,2,1,0:T(8,128)S(1)}, f32[1,1,128,128]{3,2,1,0:T(8,128)}, u32[]{:S(2)}) copy-start(f32[1,1,128,128]{3,2,1,0:T(8,128)} %param.14) | copy-start | bytes 196612
  52.5 7.7 %collective-permute-start = (f32[128,512]{1,0:T(8,128)S(1)}, f32[128,512]{1,0:T(8,128)S(1)}, u32[]{:S(2)}, u32[]{:S(2)}) collective-permute-start(f32[128,512]{1,0:T(8,128)S(1)} %bitcast.27), channel_id=1, source_target_pairs={{0,16},{16,0},{1,17},{17,1},{2,18},{18,2},{3,19},{19,3},{4,20},{20... | collective-permute-start | bytes 786440 | tf_op jit(solution)/shard_map/ppermute | solution.py:10
  54.6 6.2 %copy-start.2 = (f32[256,128]{1,0:T(8,128)S(1)}, f32[256,128]{1,0:T(8,128)}, u32[]{:S(2)}) copy-start(f32[256,128]{1,0:T(8,128)} %param.12) | copy-start | bytes 393220
  60.8 0.9 %copy-start.3 = (f32[256,128]{1,0:T(8,128)S(1)}, f32[256,128]{1,0:T(8,128)}, u32[]{:S(2)}) copy-start(f32[256,128]{1,0:T(8,128)} %param.13) | copy-start | bytes 393220
Sparse Core Ops, SparseCore 0:
  9.8 25.8 all-reduce.1
where the time goes:
time: 70.6 us; the launch traced here: 70.2 us
  waiting for transfers between devices  29.3 us (42%)
  between operations  13.5 us (19%)
  starting transfers between devices  13.1 us (19%)
  local copies, waits for them, and re-layouts  5.76 us (8%)
  matrix products  4.84 us (7%)
  other arithmetic  3.68 us (5%)
    psum x1, waiting for transfers between devices, on_device(): reduced = lax.psum(partial_value, 'quarter')  14.4 us
    all_to_all x1, waiting for transfers between devices, on_device(): lax.all_to_all(slots_one, 'grp', split_axis=0, concat_axis=0, tiled=True)  9.19 us
    all_to_all x1, starting transfers between devices, on_device(): lax.all_to_all(slots_two, 'grp', split_axis=0, concat_axis=0, tiled=True)  6.33 us
    ppermute x2, waiting for transfers between devices, swapped(): return lax.ppermute(value, axis, pairs)  5.6 us
    all_to_all x1, starting transfers between devices, on_device(): lax.all_to_all(slots_one, 'grp', split_axis=0, concat_axis=0, tiled=True)  4.74 us
    unnamed x16, local copies, waits for them, and re-layouts  2.69 us
    dot_general x2, matrix products, project(): lax.dot_general(factor, values, (((0,), (0,)), ((), ())), precision=lax.P...  2.51 us
    dot_general x4, matrix products, matmul(): jnp.dot(left, right, precision=lax.Precision.HIGHEST, preferred_element_t...  2.33 us
  transfers between devices with their start and end apart: 5, of which 3 were waited for; matrix products, arithmetic and copies ran while one was open for 10% of the time, Pallas kernels for 0%

commit v1 on v0

v1 whole, which is shorter than its diff:
```python
import functools

import jax
import jax.numpy as jnp
from jax import lax
from jax.experimental import pallas as pl
from jax.experimental.pallas import tpu as pltpu
from jax.sharding import PartitionSpec as P

AXES = ("half", "quarter", "grp")
MOST_CHIPS = 8
PARAMS = pltpu.CompilerParams(vmem_limit_bytes=16 * 2**20)
VMEM = pl.BlockSpec(memory_space=pltpu.VMEM)
SMEM = pl.BlockSpec(memory_space=pltpu.SMEM)


def f32(*shape):
    return jax.ShapeDtypeStruct(shape, jnp.float32)


def split(value):
    high = value.astype(jnp.bfloat16)
    low = (value - high.astype(jnp.float32)).astype(jnp.bfloat16)
    return high, low


def product(left, right, dims=((1,), (0,))):
    dot = functools.partial(
        lax.dot_general,
        dimension_numbers=(dims, ((), ())),
        preferred_element_type=jnp.float32,
    )
    (lh, ll), (rh, rl) = split(left), split(right)
    return dot(lh, rh) + (dot(lh, rl) + dot(ll, rh))


def coefficients(rhs, right_one, right_two):
    both = jnp.concatenate([right_one[...], right_two[...]], axis=1)
    return product(both, rhs[...], ((0,), (0,)))


def project_near(order_one, order_two, rhs, right_one, right_two, own, other, slots):
    me = lax.axis_index("grp")
    coeffs = coefficients(rhs, right_one, right_two)
    part = slots.shape[3]
    for level, order in enumerate((order_one, order_two)):
        for p in range(order.shape[2]):
            apart = order[0, 0, p] ^ me
            first = level * right_one.shape[1] + p * part
            slots[apart & 1, level, apart >> 1] = coeffs[first : first + part]
    own[...] = slots[0]
    other[...] = slots[1]


def project_far(order_one, order_two, rhs, right_one, right_two, slots_one, slots_two):
    coeffs = coefficients(rhs, right_one, right_two)
    part = slots_one.shape[1]
    for level, (order, slots) in enumerate(((order_one, slots_one), (order_two, slots_two))):
        for p in range(order.shape[2]):
            first = level * right_one.shape[1] + p * part
            slots[order[0, 0, p]] = coeffs[first : first + part]


def pair_up(own, sibling, *messages):
    chips = own.shape[1]
    for level in range(own.shape[0]):
        for apart in range(chips):
            message = messages[level * chips + apart]
            message[0] = own[level, apart]
            message[1] = sibling[level, apart]


def outer_factors(left_one, middle_one, left_two, middle_two, factors):
    rank = left_one.shape[1]
    factors[:, :rank] = product(left_one[...], middle_one[0, 0])
    factors[:, rank:] = product(left_two[...], middle_two[0, 0])


def combine(chips, factors, *refs):
    pieces, (out, stacked) = refs[:-2], refs[-2:]
    me = lax.axis_index("grp")
    rank = factors.shape[1] // 2
    part = pieces[0].shape[1]
    for apart in range(chips):
        straight, diagonal, second = (pieces[n * chips + apart] for n in range(3))
        for core in range(2):
            row = pl.multiple_of((me ^ (2 * apart + core)) * part, part)
            stacked[pl.ds(row, part)] = straight[core] + diagonal[core]
            stacked[pl.ds(rank + row, part)] = second[core]
    out[...] = product(factors[...], stacked[...])


def near(mesh, rhs, left_one, left_two, middle_one, middle_two, right_one, right_two, order_one, order_two):
    groups = mesh.shape["grp"]
    chips = groups // 2
    rank, columns = right_one.shape[1], rhs.shape[1]
    part = rank // groups

    def send(value, half=0, quarter=0, grp=0):
        sizes = [mesh.shape[axis] for axis in AXES]
        pairs = []
        for h in range(sizes[0]):
            for q in range(sizes[1]):
                for g in range(sizes[2]):
                    source = (h * sizes[1] + q) * sizes[2] + g
                    target = ((h ^ half) * sizes[1] + (q ^ quarter)) * sizes[2] + (g ^ grp)
                    pairs.append((source, target))
        return lax.ppermute(value, AXES, pairs)

    own, other = pl.pallas_call(
        project_near,
        out_shape=[f32(2, chips, part, columns)] * 2,
        in_specs=[SMEM, SMEM, VMEM, VMEM, VMEM],
        out_specs=[VMEM, VMEM],
        scratch_shapes=[pltpu.VMEM((2, 2, chips, part, columns), jnp.float32)],
        compiler_params=PARAMS,
    )(order_one, order_two, rhs, right_one, right_two)
    factors = pl.pallas_call(
        outer_factors,
        out_shape=f32(left_one.shape[0], 2 * rank),
        in_specs=[VMEM] * 4,
        out_specs=VMEM,
        compiler_params=PARAMS,
    )(left_one, middle_one, left_two, middle_two)
    sibling = send(other, grp=1)
    messages = pl.pallas_call(
        pair_up,
        out_shape=[f32(2, part, columns)] * (2 * chips),
        in_specs=[VMEM, VMEM],
        out_specs=[VMEM] * (2 * chips),
        compiler_params=PARAMS,
    )(own, sibling)
    straight = [send(messages[k], half=1, grp=2 * k) for k in range(chips)]
    second = [send(messages[chips + k], quarter=1, grp=2 * k) for k in range(chips)]
    diagonal = [send(value, quarter=1) for value in straight]
    return pl.pallas_call(
        functools.partial(combine, chips),
        out_shape=f32(left_one.shape[0], columns),
        in_specs=[VMEM] * (1 + 3 * chips),
        out_specs=VMEM,
        scratch_shapes=[pltpu.VMEM((2 * rank, columns), jnp.float32)],
        compiler_params=PARAMS,
    )(factors, *straight, *diagonal, *second)


def far(mesh, rhs, left_one, left_two, middle_one, middle_two, right_one, right_two, order_one, order_two):
    groups = mesh.shape["grp"]
    rank, columns = right_one.shape[1], rhs.shape[1]
    slots = pl.pallas_call(
        project_far,
        out_shape=[f32(groups, rank // groups, columns)] * 2,
        in_specs=[SMEM, SMEM, VMEM, VMEM, VMEM],
        out_specs=[VMEM, VMEM],
        compiler_params=PARAMS,
    )(order_one, order_two, rhs, right_one, right_two)
    swap = [(0, 1), (1, 0)]
    first, second = (
        lax.all_to_all(value, "grp", 0, 0, tiled=True).reshape(rank, columns) for value in slots
    )
    first = lax.ppermute(first, "half", swap)
    first = first + lax.ppermute(first, "quarter", swap)
    second = lax.ppermute(second, "quarter", swap)
    dot = functools.partial(jnp.dot, precision=lax.Precision.HIGHEST)
    result = dot(left_one, dot(middle_one[0, 0], first))
    return result + dot(left_two, dot(middle_two[0, 0], second))


def solution(mesh):
    in_specs = (
        P(AXES, None),
        P(AXES, None),
        P(AXES, None),
        P("half", "grp", None, None),
        P(("half", "quarter"), "grp", None, None),
        P(AXES, None),
        P(AXES, None),
        P("half", "grp", None),
        P(("half", "quarter"), "grp", None),
    )
    groups = mesh.shape["grp"]
    direct = groups % 2 == 0 and groups & (groups - 1) == 0 and groups // 2 <= MOST_CHIPS
    return jax.shard_map(
        functools.partial(near if direct else far, mesh),
        mesh=mesh,
        in_specs=in_specs,
        out_specs=P(AXES, None),
        check_vma=False,
    )
```

time: 70.6 us -> 32.5 us (0.46)
  waiting for transfers between devices: 29.3 us -> 3.92 us
  between operations: 13.5 us -> 0.05 us
  starting transfers between devices: 13.1 us -> 21.7 us
  matrix products: 4.84 us -> 0 us
  other arithmetic: 3.68 us -> 0 us
  Pallas kernels: 0 us -> 2.52 us
  local copies, waits for them, and re-layouts: 5.76 us -> 4.17 us
    ppermute x2 -> x13, starting transfers between devices: 2.02 us -> 21.7 us  [send(): return lax.ppermute(value, AXES, pairs)]
    psum x1 -> x0, waiting for transfers between devices: 14.4 us -> none  [on_device(): reduced = lax.psum(partial_value, 'quarter')]
    all_to_all x2 -> x0, starting transfers between devices: 11.1 us -> none  [the longest x1 6.33 us: on_device(): lax.all_to_all(slots_two, 'grp', split_axis=0, concat_axis=0, tiled=True)]
    all_to_all x2 -> x0, waiting for transfers between devices: 9.19 us -> none  [the longest x1 9.19 us: on_device(): lax.all_to_all(slots_one, 'grp', split_axis=0, concat_axis=0, tiled=True)]
    dot_general x6 -> x0, matrix products: 4.84 us -> none  [the longest x2 2.51 us: project(): lax.dot_general(factor, values, (((0,), (0,)), ((), ())), precision=lax.P...]
    pallas_call x0 -> x4, Pallas kernels: none -> 2.52 us  [the longest x1 1.24 us: near(): pl.pallas_call(functools.partial(combine, chips), out_shape=f32(left_one....]
    gather x2 -> x0, local copies, waits for them, and re-layouts: 2.08 us -> none  [to_slots(): return jnp.take(parts, jnp.argsort(order), axis=0)]
    sort x2 -> x0, other arithmetic: 2.06 us -> none  [to_slots(): return jnp.take(parts, jnp.argsort(order), axis=0)]
  transfers between devices with their start and end apart: 5 -> 13, of which waited for: 3 -> 6; matrix products, arithmetic and copies ran while one was open for 10% -> 0% of each run, Pallas kernels for 0% -> 1%
where the time goes in v1:
time: 32.5 us; the launch traced here: 32.3 us
  starting transfers between devices  21.7 us (67%)
  local copies, waits for them, and re-layouts  4.17 us (13%)
  waiting for transfers between devices  3.92 us (12%)
  Pallas kernels  2.52 us (8%)
    ppermute x13, starting transfers between devices, send(): return lax.ppermute(value, AXES, pairs)  21.7 us
    unnamed x18, local copies, waits for them, and re-layouts  4.17 us
    ppermute x13, waiting for transfers between devices, send(): return lax.ppermute(value, AXES, pairs)  3.92 us
    pallas_call x1, Pallas kernels, near(): pl.pallas_call(functools.partial(combine, chips), out_shape=f32(left_one....  1.24 us
    pallas_call x1, Pallas kernels, near(): pl.pallas_call(project_near, out_shape=[f32(2, chips, part, columns)] * 2...  1 us
  transfers between devices with their start and end apart: 13, of which 6 were waited for; matrix products, arithmetic and copies ran while one was open for 0% of the time, Pallas kernels for 1%

profile of v1, /device:TPU:0, one launch (start us, length us, event | category | flops | bytes accessed | tf_op | source)
XLA Modules:
  0.0 32.3 jit_solution(2253690481675092778)
XLA Ops:
  0.0 0.0 copy-start
  0.0 1.0 %copy-done = f32[256,512]{1,0:T(8,128)S(1)} copy-done((f32[256,512]{1,0:T(8,128)S(1)}, f32[256,512]{1,0:T(8,128)}, u32[]{:S(2)}) %copy-start) | copy-done | bytes 524312
  1.0 0.0 copy-start.3
  1.0 0.9 %copy-done.3 = f32[256,128]{1,0:T(8,128)S(1)} copy-done((f32[256,128]{1,0:T(8,128)S(1)}, f32[256,128]{1,0:T(8,128)}, u32[]{:S(2)}) %copy-start.3) | copy-done | bytes 131096
  1.9 0.0 copy-start.4
  1.9 0.9 %copy-done.4 = f32[256,128]{1,0:T(8,128)S(1)} copy-done((f32[256,128]{1,0:T(8,128)S(1)}, f32[256,128]{1,0:T(8,128)}, u32[]{:S(2)}) %copy-start.4) | copy-done | bytes 131096
  2.9 0.0 copy-start.7
  2.9 0.7 %copy-done.7 = s32[1,1,8]{2,1,0:T(1,128)S(1)} copy-done((s32[1,1,8]{2,1,0:T(1,128)S(1)}, s32[1,1,8]{2,1,0:T(1,128)}, u32[]{:S(2)}) %copy-start.7) | copy-done | bytes 56
  3.5 0.0 copy-start.8
  3.5 0.7 %copy-done.8 = s32[1,1,8]{2,1,0:T(1,128)S(1)} copy-done((s32[1,1,8]{2,1,0:T(1,128)S(1)}, s32[1,1,8]{2,1,0:T(1,128)}, u32[]{:S(2)}) %copy-start.8) | copy-done | bytes 56
  4.2 1.0 %shard_map.92 = (f32[2,4,16,512]{3,2,1,0:T(8,128)S(1)}, f32[2,4,16,512]{3,2,1,0:T(8,128)S(1)}) custom-call(s32[1,1,8]{2,1,0:T(1,128)S(1)} %copy-done.7, s32[1,1,8]{2,1,0:T(1,128)S(1)} %copy-done.8, f32[256,512]{1,0:T(8,128)S(1)} %copy-done, f32[256,128]{1,0:T(8,128)S(1)} %copy-done.3, f32[256,128]{1,0:T(8,128)S(1)} %copy-done.4), custom_call_target="tpu_custom_call" | custom-call | tf_op jit(solution)/shard_map/pallas_call | solution.py:110
  5.2 0.5 %collective-permute-start = (f32[2,4,16,512]{3,2,1,0:T(8,128)S(1)}, f32[2,4,16,512]{3,2,1,0:T(8,128)S(1)}, u32[]{:S(2)}, u32[]{:S(2)}) collective-permute-start(f32[2,4,16,512]{3,2,1,0:T(8,128)S(1)} %get-tuple-element.16), channel_id=1, source_target_pairs={{0,1},{1,0},{2,3},{3,2},{4,5},{5,4},{6,7},{7,6},{8,9},{9,8},{10,11... | collective-permute-start | bytes 786440 | tf_op jit(solution)/shard_map/ppermute | solution.py:108
  5.7 1.2 %collective-permute-done.sibling = f32[2,4,16,512]{3,2,1,0:T(8,128)S(1)} collective-permute-done((f32[2,4,16,512]{3,2,1,0:T(8,128)S(1)}, f32[2,4,16,512]{3,2,1,0:T(8,128)S(1)}, u32[]{:S(2)}, u32[]{:S(2)}) %collective-permute-start) | collective-permute-done | bytes 262176 | tf_op jit(solution)/shard_map/ppermute | solution.py:108
  6.8 0.0 copy-start.1
  6.9 0.0 copy-start.2
  6.9 0.0 copy-start.5
  6.9 0.0 copy-start.6
  6.9 2.9 %collective-permute-start.1 = (f32[2,16,512]{2,1,0:T(8,128)S(1)}, f32[2,16,512]{2,1,0:T(8,128)S(1)}, u32[]{:S(2)}, u32[]{:S(2)}) collective-permute-start(f32[2,16,512]{2,1,0:T(8,128)S(1)} %get-tuple-element.17), channel_id=1, source_target_pairs={{0,16},{1,17},{2,18},{3,19},{4,20},{5,21},{6,22},{7,23},{8,24},{9,... | collective-permute-start | bytes 196616 | tf_op jit(solution)/shard_map/ppermute | solution.py:108
  9.8 1.6 %collective-permute-start.2 = (f32[2,16,512]{2,1,0:T(8,128)S(1)}, f32[2,16,512]{2,1,0:T(8,128)S(1)}, u32[]{:S(2)}, u32[]{:S(2)}) collective-permute-start(f32[2,16,512]{2,1,0:T(8,128)S(1)} %get-tuple-element.18), channel_id=1, source_target_pairs={{0,18},{1,19},{2,16},{3,17},{4,22},{5,23},{6,20},{7,21},{8,26},{9,... | collective-permute-start | bytes 196616 | tf_op jit(solution)/shard_map/ppermute | solution.py:108
  11.4 3.5 %collective-permute-start.3 = (f32[2,16,512]{2,1,0:T(8,128)S(1)}, f32[2,16,512]{2,1,0:T(8,128)S(1)}, u32[]{:S(2)}, u32[]{:S(2)}) collective-permute-start(f32[2,16,512]{2,1,0:T(8,128)S(1)} %get-tuple-element.19), channel_id=1, source_target_pairs={{0,20},{1,21},{2,22},{3,23},{4,16},{5,17},{6,18},{7,19},{8,28},{9,... | collective-permute-start | bytes 196616 | tf_op jit(solution)/shard_map/ppermute | solution.py:108
  14.9 0.0 collective-permute-start.4
  14.9 1.7 %collective-permute-start.9 = (f32[2,16,512]{2,1,0:T(8,128)S(1)}, f32[2,16,512]{2,1,0:T(8,128)S(1)}, u32[]{:S(2)}, u32[]{:S(2)}) collective-permute-start(f32[2,16,512]{2,1,0:T(8,128)S(1)} %get-tuple-element.21), channel_id=1, source_target_pairs={{0,8},{1,9},{2,10},{3,11},{4,12},{5,13},{6,14},{7,15},{8,0},{9,1},... | collective-permute-start | bytes 196616 | tf_op jit(solution)/shard_map/ppermute | solution.py:108
  16.6 0.0 collective-permute-done.1.refs_0_
  16.6 0.6 %collective-permute-start.10 = (f32[2,16,512]{2,1,0:T(8,128)S(1)}, f32[2,16,512]{2,1,0:T(8,128)S(1)}, u32[]{:S(2)}, u32[]{:S(2)}) collective-permute-start(f32[2,16,512]{2,1,0:T(8,128)S(1)} %get-tuple-element.22), channel_id=1, source_target_pairs={{0,10},{1,11},{2,8},{3,9},{4,14},{5,15},{6,12},{7,13},{8,2},{9,3},... | collective-permute-start | bytes 196616 | tf_op jit(solution)/shard_map/ppermute | solution.py:108
  17.2 0.0 collective-permute-done.2.refs_1_
  17.2 4.4 %collective-permute-start.11 = (f32[2,16,512]{2,1,0:T(8,128)S(1)}, f32[2,16,512]{2,1,0:T(8,128)S(1)}, u32[]{:S(2)}, u32[]{:S(2)}) collective-permute-start(f32[2,16,512]{2,1,0:T(8,128)S(1)} %get-tuple-element.23), channel_id=1, source_target_pairs={{0,12},{1,13},{2,14},{3,15},{4,8},{5,9},{6,10},{7,11},{8,4},{9,5},... | collective-permute-start | bytes 196616 | tf_op jit(solution)/shard_map/ppermute | solution.py:108
  21.7 0.0 collective-permute-done.3.refs_2_
  21.7 2.3 %collective-permute-start.12 = (f32[2,16,512]{2,1,0:T(8,128)S(1)}, f32[2,16,512]{2,1,0:T(8,128)S(1)}, u32[]{:S(2)}, u32[]{:S(2)}) collective-permute-start(f32[2,16,512]{2,1,0:T(8,128)S(1)} %get-tuple-element.24), channel_id=1, source_target_pairs={{0,14},{1,15},{2,12},{3,13},{4,10},{5,11},{6,8},{7,9},{8,6},{9,7},... | collective-permute-start | bytes 196616 | tf_op jit(solution)/shard_map/ppermute | solution.py:108
  24.0 0.0 collective-permute-done.4.refs_3_
  24.0 0.5 %collective-permute-start.5 = (f32[2,16,512]{2,1,0:T(8,128)S(1)}, f32[2,16,512]{2,1,0:T(8,128)S(1)}, u32[]{:S(2)}, u32[]{:S(2)}) collective-permute-start(f32[2,16,512]{2,1,0:T(8,128)S(1)} %collective-permute-done.1.refs_0_), channel_id=1, source_target_pairs={{0,8},{1,9},{2,10},{3,11},{4,12},{5,13},{6,14},{7,15},{8,0},{9,1},... | collective-permute-start | bytes 196616 | tf_op jit(solution)/shard_map/ppermute | solution.py:108
  24.5 0.0 collective-permute-done.9.refs_8_
  24.5 1.5 %collective-permute-start.6 = (f32[2,16,512]{2,1,0:T(8,128)S(1)}, f32[2,16,512]{2,1,0:T(8,128)S(1)}, u32[]{:S(2)}, u32[]{:S(2)}) collective-permute-start(f32[2,16,512]{2,1,0:T(8,128)S(1)} %collective-permute-done.2.refs_1_), channel_id=1, source_target_pairs={{0,8},{1,9},{2,10},{3,11},{4,12},{5,13},{6,14},{7,15},{8,0},{9,1},... | collective-permute-start | bytes 196616 | tf_op jit(solution)/shard_map/ppermute | solution.py:108
  26.0 0.0 collective-permute-done.10.refs_9_
  26.0 0.5 %collective-permute-start.7 = (f32[2,16,512]{2,1,0:T(8,128)S(1)}, f32[2,16,512]{2,1,0:T(8,128)S(1)}, u32[]{:S(2)}, u32[]{:S(2)}) collective-permute-start(f32[2,16,512]{2,1,0:T(8,128)S(1)} %collective-permute-done.3.refs_2_), channel_id=1, source_target_pairs={{0,8},{1,9},{2,10},{3,11},{4,12},{5,13},{6,14},{7,15},{8,0},{9,1},... | collective-permute-start | bytes 196616 | tf_op jit(solution)/shard_map/ppermute | solution.py:108
  26.6 0.0 collective-permute-done.11.refs_10_
  26.6 1.5 %collective-permute-start.8 = (f32[2,16,512]{2,1,0:T(8,128)S(1)}, f32[2,16,512]{2,1,0:T(8,128)S(1)}, u32[]{:S(2)}, u32[]{:S(2)}) collective-permute-start(f32[2,16,512]{2,1,0:T(8,128)S(1)} %collective-permute-done.4.refs_3_), channel_id=1, source_target_pairs={{0,8},{1,9},{2,10},{3,11},{4,12},{5,13},{6,14},{7,15},{8,0},{9,1},... | collective-permute-start | bytes 196616 | tf_op jit(solution)/shard_map/ppermute | solution.py:108
  28.1 0.0 copy-done.1
  28.1 0.0 copy-done.2
  28.1 0.0 copy-done.5
  28.1 0.0 copy-done.6
  28.1 0.3 shard_map.91.factors
  28.3 0.4 %collective-permute-done.12.refs_11_ = f32[2,16,512]{2,1,0:T(8,128)S(1)} collective-permute-done((f32[2,16,512]{2,1,0:T(8,128)S(1)}, f32[2,16,512]{2,1,0:T(8,128)S(1)}, u32[]{:S(2)}, u32[]{:S(2)}) %collective-permute-start.12) | collective-permute-done | bytes 65568 | tf_op jit(solution)/shard_map/ppermute | solution.py:108
  28.8 0.2 collective-permute-done.5.refs_4_
  29.0 0.7 %collective-permute-done.6.refs_5_ = f32[2,16,512]{2,1,0:T(8,128)S(1)} collective-permute-done((f32[2,16,512]{2,1,0:T(8,128)S(1)}, f32[2,16,512]{2,1,0:T(8,128)S(1)}, u32[]{:S(2)}, u32[]{:S(2)}) %collective-permute-start.6) | collective-permute-done | bytes 65568 | tf_op jit(solution)/shard_map/ppermute | solution.py:108
  29.7 0.7 %collective-permute-done.7.refs_6_ = f32[2,16,512]{2,1,0:T(8,128)S(1)} collective-permute-done((f32[2,16,512]{2,1,0:T(8,128)S(1)}, f32[2,16,512]{2,1,0:T(8,128)S(1)}, u32[]{:S(2)}, u32[]{:S(2)}) %collective-permute-start.7) | collective-permute-done | bytes 65568 | tf_op jit(solution)/shard_map/ppermute | solution.py:108
  30.4 0.7 %collective-permute-done.8.refs_7_ = f32[2,16,512]{2,1,0:T(8,128)S(1)} collective-permute-done((f32[2,16,512]{2,1,0:T(8,128)S(1)}, f32[2,16,512]{2,1,0:T(8,128)S(1)}, u32[]{:S(2)}, u32[]{:S(2)}) %collective-permute-start.8) | collective-permute-done | bytes 65568 | tf_op jit(solution)/shard_map/ppermute | solution.py:108
  31.1 1.2 %shard_map.94 = f32[256,512]{1,0:T(8,128)} custom-call(f32[256,256]{1,0:T(8,128)S(1)} %shard_map.91.factors, f32[2,16,512]{2,1,0:T(8,128)S(1)} %collective-permute-done.1.refs_0_, f32[2,16,512]{2,1,0:T(8,128)S(1)} %collective-permute-done.2.refs_1_, f32[2,16,512]{2,1,0:T(8,128)S(1)} %collective-permute-done.3.refs_2_, ...), custom_call_target="tpu_custom_call" | custom-call | tf_op jit(solution)/shard_map/pallas_call | solution.py:136
  (1 shorter events, 0.0 us)
Async XLA Ops:
  0.0 1.0 %copy-start = (f32[256,512]{1,0:T(8,128)S(1)}, f32[256,512]{1,0:T(8,128)}, u32[]{:S(2)}) copy-start(f32[256,512]{1,0:T(8,128)} %rhs.1) | copy-start | bytes 1572868
  1.0 0.9 %copy-start.3 = (f32[256,128]{1,0:T(8,128)S(1)}, f32[256,128]{1,0:T(8,128)}, u32[]{:S(2)}) copy-start(f32[256,128]{1,0:T(8,128)} %right_one.1) | copy-start | bytes 393220
  1.9 0.9 %copy-start.4 = (f32[256,128]{1,0:T(8,128)S(1)}, f32[256,128]{1,0:T(8,128)}, u32[]{:S(2)}) copy-start(f32[256,128]{1,0:T(8,128)} %right_two.1) | copy-start | bytes 393220
  2.9 0.7 %copy-start.7 = (s32[1,1,8]{2,1,0:T(1,128)S(1)}, s32[1,1,8]{2,1,0:T(1,128)}, u32[]{:S(2)}) copy-start(s32[1,1,8]{2,1,0:T(1,128)} %order_one.1) | copy-start | bytes 100
  3.5 0.7 %copy-start.8 = (s32[1,1,8]{2,1,0:T(1,128)S(1)}, s32[1,1,8]{2,1,0:T(1,128)}, u32[]{:S(2)}) copy-start(s32[1,1,8]{2,1,0:T(1,128)} %order_two.1) | copy-start | bytes 100
  5.2 1.7 %collective-permute-start = (f32[2,4,16,512]{3,2,1,0:T(8,128)S(1)}, f32[2,4,16,512]{3,2,1,0:T(8,128)S(1)}, u32[]{:S(2)}, u32[]{:S(2)}) collective-permute-start(f32[2,4,16,512]{3,2,1,0:T(8,128)S(1)} %get-tuple-element.16), channel_id=1, source_target_pairs={{0,1},{1,0},{2,3},{3,2},{4,5},{5,4},{6,7},{7,6},{8,9},{9,8},{10,11... | collective-permute-start | bytes 786440 | tf_op jit(solution)/shard_map/ppermute | solution.py:108
  6.8 21.2 %copy-start.1 = (f32[256,128]{1,0:T(8,128)S(1)}, f32[256,128]{1,0:T(8,128)}, u32[]{:S(2)}) copy-start(f32[256,128]{1,0:T(8,128)} %left_one.1) | copy-start | bytes 393220
  6.9 21.2 %copy-start.2 = (f32[256,128]{1,0:T(8,128)S(1)}, f32[256,128]{1,0:T(8,128)}, u32[]{:S(2)}) copy-start(f32[256,128]{1,0:T(8,128)} %left_two.1) | copy-start | bytes 393220
  6.9 21.2 %copy-start.5 = (f32[1,1,128,128]{3,2,1,0:T(8,128)S(1)}, f32[1,1,128,128]{3,2,1,0:T(8,128)}, u32[]{:S(2)}) copy-start(f32[1,1,128,128]{3,2,1,0:T(8,128)} %middle_one.1) | copy-start | bytes 196612
  6.9 21.2 %copy-start.6 = (f32[1,1,128,128]{3,2,1,0:T(8,128)S(1)}, f32[1,1,128,128]{3,2,1,0:T(8,128)}, u32[]{:S(2)}) copy-start(f32[1,1,128,128]{3,2,1,0:T(8,128)} %middle_two.1) | copy-start | bytes 196612
  6.9 9.7 %collective-permute-start.1 = (f32[2,16,512]{2,1,0:T(8,128)S(1)}, f32[2,16,512]{2,1,0:T(8,128)S(1)}, u32[]{:S(2)}, u32[]{:S(2)}) collective-permute-start(f32[2,16,512]{2,1,0:T(8,128)S(1)} %get-tuple-element.17), channel_id=1, source_target_pairs={{0,16},{1,17},{2,18},{3,19},{4,20},{5,21},{6,22},{7,23},{8,24},{9,... | collective-permute-start | bytes 196616 | tf_op jit(solution)/shard_map/ppermute | solution.py:108
  9.8 7.4 %collective-permute-start.2 = (f32[2,16,512]{2,1,0:T(8,128)S(1)}, f32[2,16,512]{2,1,0:T(8,128)S(1)}, u32[]{:S(2)}, u32[]{:S(2)}) collective-permute-start(f32[2,16,512]{2,1,0:T(8,128)S(1)} %get-tuple-element.18), channel_id=1, source_target_pairs={{0,18},{1,19},{2,16},{3,17},{4,22},{5,23},{6,20},{7,21},{8,26},{9,... | collective-permute-start | bytes 196616 | tf_op jit(solution)/shard_map/ppermute | solution.py:108
  11.4 10.3 %collective-permute-start.3 = (f32[2,16,512]{2,1,0:T(8,128)S(1)}, f32[2,16,512]{2,1,0:T(8,128)S(1)}, u32[]{:S(2)}, u32[]{:S(2)}) collective-permute-start(f32[2,16,512]{2,1,0:T(8,128)S(1)} %get-tuple-element.19), channel_id=1, source_target_pairs={{0,20},{1,21},{2,22},{3,23},{4,16},{5,17},{6,18},{7,19},{8,28},{9,... | collective-permute-start | bytes 196616 | tf_op jit(solution)/shard_map/ppermute | solution.py:108
  14.9 9.1 %collective-permute-start.4 = (f32[2,16,512]{2,1,0:T(8,128)S(1)}, f32[2,16,512]{2,1,0:T(8,128)S(1)}, u32[]{:S(2)}, u32[]{:S(2)}) collective-permute-start(f32[2,16,512]{2,1,0:T(8,128)S(1)} %get-tuple-element.20), channel_id=1, source_target_pairs={{0,22},{1,23},{2,20},{3,21},{4,18},{5,19},{6,16},{7,17},{8,30},{9,... | collective-permute-start | bytes 196616 | tf_op jit(solution)/shard_map/ppermute | solution.py:108
  14.9 9.6 %collective-permute-start.9 = (f32[2,16,512]{2,1,0:T(8,128)S(1)}, f32[2,16,512]{2,1,0:T(8,128)S(1)}, u32[]{:S(2)}, u32[]{:S(2)}) collective-permute-start(f32[2,16,512]{2,1,0:T(8,128)S(1)} %get-tuple-element.21), channel_id=1, source_target_pairs={{0,8},{1,9},{2,10},{3,11},{4,12},{5,13},{6,14},{7,15},{8,0},{9,1},... | collective-permute-start | bytes 196616 | tf_op jit(solution)/shard_map/ppermute | solution.py:108
  16.6 9.4 %collective-permute-start.10 = (f32[2,16,512]{2,1,0:T(8,128)S(1)}, f32[2,16,512]{2,1,0:T(8,128)S(1)}, u32[]{:S(2)}, u32[]{:S(2)}) collective-permute-start(f32[2,16,512]{2,1,0:T(8,128)S(1)} %get-tuple-element.22), channel_id=1, source_target_pairs={{0,10},{1,11},{2,8},{3,9},{4,14},{5,15},{6,12},{7,13},{8,2},{9,3},... | collective-permute-start | bytes 196616 | tf_op jit(solution)/shard_map/ppermute | solution.py:108
  17.2 9.3 %collective-permute-start.11 = (f32[2,16,512]{2,1,0:T(8,128)S(1)}, f32[2,16,512]{2,1,0:T(8,128)S(1)}, u32[]{:S(2)}, u32[]{:S(2)}) collective-permute-start(f32[2,16,512]{2,1,0:T(8,128)S(1)} %get-tuple-element.23), channel_id=1, source_target_pairs={{0,12},{1,13},{2,14},{3,15},{4,8},{5,9},{6,10},{7,11},{8,4},{9,5},... | collective-permute-start | bytes 196616 | tf_op jit(solution)/shard_map/ppermute | solution.py:108
  21.7 7.1 %collective-permute-start.12 = (f32[2,16,512]{2,1,0:T(8,128)S(1)}, f32[2,16,512]{2,1,0:T(8,128)S(1)}, u32[]{:S(2)}, u32[]{:S(2)}) collective-permute-start(f32[2,16,512]{2,1,0:T(8,128)S(1)} %get-tuple-element.24), channel_id=1, source_target_pairs={{0,14},{1,15},{2,12},{3,13},{4,10},{5,11},{6,8},{7,9},{8,6},{9,7},... | collective-permute-start | bytes 196616 | tf_op jit(solution)/shard_map/ppermute | solution.py:108
  24.0 5.0 %collective-permute-start.5 = (f32[2,16,512]{2,1,0:T(8,128)S(1)}, f32[2,16,512]{2,1,0:T(8,128)S(1)}, u32[]{:S(2)}, u32[]{:S(2)}) collective-permute-start(f32[2,16,512]{2,1,0:T(8,128)S(1)} %collective-permute-done.1.refs_0_), channel_id=1, source_target_pairs={{0,8},{1,9},{2,10},{3,11},{4,12},{5,13},{6,14},{7,15},{8,0},{9,1},... | collective-permute-start | bytes 196616 | tf_op jit(solution)/shard_map/ppermute | solution.py:108
  24.5 5.2 %collective-permute-start.6 = (f32[2,16,512]{2,1,0:T(8,128)S(1)}, f32[2,16,512]{2,1,0:T(8,128)S(1)}, u32[]{:S(2)}, u32[]{:S(2)}) collective-permute-start(f32[2,16,512]{2,1,0:T(8,128)S(1)} %collective-permute-done.2.refs_1_), channel_id=1, source_target_pairs={{0,8},{1,9},{2,10},{3,11},{4,12},{5,13},{6,14},{7,15},{8,0},{9,1},... | collective-permute-start | bytes 196616 | tf_op jit(solution)/shard_map/ppermute | solution.py:108
  26.0 4.3 %collective-permute-start.7 = (f32[2,16,512]{2,1,0:T(8,128)S(1)}, f32[2,16,512]{2,1,0:T(8,128)S(1)}, u32[]{:S(2)}, u32[]{:S(2)}) collective-permute-start(f32[2,16,512]{2,1,0:T(8,128)S(1)} %collective-permute-done.3.refs_2_), channel_id=1, source_target_pairs={{0,8},{1,9},{2,10},{3,11},{4,12},{5,13},{6,14},{7,15},{8,0},{9,1},... | collective-permute-start | bytes 196616 | tf_op jit(solution)/shard_map/ppermute | solution.py:108
  26.6 4.5 %collective-permute-start.8 = (f32[2,16,512]{2,1,0:T(8,128)S(1)}, f32[2,16,512]{2,1,0:T(8,128)S(1)}, u32[]{:S(2)}, u32[]{:S(2)}) collective-permute-start(f32[2,16,512]{2,1,0:T(8,128)S(1)} %collective-permute-done.4.refs_3_), channel_id=1, source_target_pairs={{0,8},{1,9},{2,10},{3,11},{4,12},{5,13},{6,14},{7,15},{8,0},{9,1},... | collective-permute-start | bytes 196616 | tf_op jit(solution)/shard_map/ppermute | solution.py:108

commit v2 on v1

v2 whole, which is shorter than its diff:
```python
import functools

import jax
import jax.numpy as jnp
from jax import lax
from jax.experimental import pallas as pl
from jax.experimental.pallas import tpu as pltpu
from jax.sharding import PartitionSpec as P

AXES = ("half", "quarter", "grp")
MOST_CHIPS = 8
PARAMS = pltpu.CompilerParams(vmem_limit_bytes=16 * 2**20)
VMEM = pl.BlockSpec(memory_space=pltpu.VMEM)
HBM = pl.BlockSpec(memory_space=pltpu.HBM)
SMEM = pl.BlockSpec(memory_space=pltpu.SMEM)


def f32(*shape):
    return jax.ShapeDtypeStruct(shape, jnp.float32)


def in_hbm(value):
    return pltpu.with_memory_space_constraint(value, pltpu.HBM)


def split(value):
    high = value.astype(jnp.bfloat16)
    low = (value - high.astype(jnp.float32)).astype(jnp.bfloat16)
    return high, low


def product(left, right, dims=((1,), (0,))):
    dot = functools.partial(
        lax.dot_general,
        dimension_numbers=(dims, ((), ())),
        preferred_element_type=jnp.float32,
    )
    (lh, ll), (rh, rl) = split(left), split(right)
    return dot(lh, rh) + (dot(lh, rl) + dot(ll, rh))


def project_one(
    order_one, order_two, rhs, right_one, right_two,
    own, other, rhs_here, right_here, order_here,
    slots, right, orders, sems,
):
    copies = [
        pltpu.make_async_copy(*pair, sems.at[n])
        for n, pair in enumerate(
            (
                (right_one, right),
                (rhs, rhs_here),
                (order_one, orders),
                (right_two, right_here),
                (order_two, order_here),
            )
        )
    ]
    for copy in copies:
        copy.start()
    me = lax.axis_index("grp")
    for copy in copies[:3]:
        copy.wait()
    coeffs = product(right[...], rhs_here[...], ((0,), (0,)))
    part = slots.shape[2]
    for p in range(orders.shape[2]):
        apart = orders[0, 0, p] ^ me
        slots[apart & 1, apart >> 1] = coeffs[p * part : (p + 1) * part]
    own[...] = slots[0]
    other[...] = slots[1]
    for copy in copies[3:]:
        copy.wait()


def project_two(order, rhs, right, own, other, slots):
    me = lax.axis_index("grp")
    coeffs = product(right[...], rhs[...], ((0,), (0,)))
    part = slots.shape[3]
    for p in range(order.shape[2]):
        receiver = order[0, 0, p]
        apart = (receiver >> 1) ^ (me >> 1)
        slots[(apart ^ me) & 1, apart >> 1, receiver & 1] = coeffs[p * part : (p + 1) * part]
    own[...] = slots[0]
    other[...] = slots[1]


def pair_one(own, sibling, *messages):
    for apart, message in enumerate(messages):
        message[0] = own[apart]
        message[1] = sibling[apart]


def pair_two(own, sibling, *messages):
    for n, message in enumerate(messages):
        message[0] = own[n]
        message[1] = sibling[n]


def pack(*refs):
    out = refs[-1]
    for n, ref in enumerate(refs[:-1]):
        out[n] = ref[...]


def pack_other(*refs):
    out = refs[-1]
    there = 1 - (lax.axis_index("grp") & 1)
    for n, ref in enumerate(refs[:-1]):
        out[n] = ref[:, there]


def outer_factors(left_one, middle_one, left_two, middle_two, factors):
    rank = left_one.shape[1]
    factors[:, :rank] = product(left_one[...], middle_one[0, 0])
    factors[:, rank:] = product(left_two[...], middle_two[0, 0])


def combine(chips, factors, *refs):
    straight, refs = refs[:chips], refs[chips:]
    diagonal, refs = refs[:2], refs[2:]
    second, refs = refs[: chips // 2], refs[chips // 2 :]
    sibling, out, stacked = refs
    me = lax.axis_index("grp")
    core = me & 1
    rank = factors.shape[1] // 2
    part = sibling.shape[2]

    def put(group, level, rows):
        stacked[pl.ds(pl.multiple_of(level * rank + group * part, part), part)] = rows

    for apart in range(chips):
        for other in range(2):
            rows = straight[apart][other] + diagonal[apart // (chips // 2)][apart % (chips // 2), other]
            put(me ^ (2 * apart + other), 0, rows)
    for n in range(chips // 2):
        for other in range(2):
            put(me ^ (2 * (2 * n + core) + other), 1, second[n][other, core])
            put(me ^ (2 * (2 * n + 1 - core) + 1 - other), 1, sibling[n, other])
    out[...] = product(factors[...], stacked[...])


def near(mesh, rhs, left_one, left_two, middle_one, middle_two, right_one, right_two, order_one, order_two):
    groups = mesh.shape["grp"]
    chips = groups // 2
    rank, columns = right_one.shape[1], rhs.shape[1]
    part = rank // groups
    call = functools.partial(pl.pallas_call, compiler_params=PARAMS)

    def send(value, half=0, quarter=0, grp=lambda g: g):
        sizes = [mesh.shape[axis] for axis in AXES]
        pairs = []
        for h in range(sizes[0]):
            for q in range(sizes[1]):
                for g in range(sizes[2]):
                    source = (h * sizes[1] + q) * sizes[2] + g
                    target = ((h ^ half) * sizes[1] + (q ^ quarter)) * sizes[2] + grp(g)
                    pairs.append((source, target))
        return lax.ppermute(value, AXES, pairs)

    own_one, other_one, rhs_here, right_here, order_here = call(
        project_one,
        out_shape=[
            f32(chips, part, columns),
            f32(chips, part, columns),
            rhs,
            right_two,
            order_two,
        ],
        in_specs=[HBM] * 5,
        out_specs=[VMEM] * 4 + [SMEM],
        scratch_shapes=[
            pltpu.VMEM((2, chips, part, columns), jnp.float32),
            pltpu.VMEM(right_one.shape, jnp.float32),
            pltpu.SMEM(order_one.shape, jnp.int32),
            pltpu.SemaphoreType.DMA((5,)),
        ],
    )(*(in_hbm(x) for x in (order_one, order_two, rhs, right_one, right_two)))
    sibling_one = send(other_one, grp=lambda g: g ^ 1)
    own_two, other_two = call(
        project_two,
        out_shape=[f32(chips // 2, 2, part, columns)] * 2,
        in_specs=[SMEM, VMEM, VMEM],
        out_specs=[VMEM, VMEM],
        scratch_shapes=[pltpu.VMEM((2, chips // 2, 2, part, columns), jnp.float32)],
    )(order_here, rhs_here, right_here)
    sibling_two = send(other_two, grp=lambda g: g ^ 1)
    messages_one = call(
        pair_one,
        out_shape=[f32(2, part, columns)] * chips,
        in_specs=[VMEM, VMEM],
        out_specs=[VMEM] * chips,
    )(own_one, sibling_one)
    straight = [send(messages_one[k], half=1, grp=lambda g, k=k: g ^ (2 * k)) for k in range(chips)]
    messages_two = call(
        pair_two,
        out_shape=[f32(2, 2, part, columns)] * (chips // 2),
        in_specs=[VMEM, VMEM],
        out_specs=[VMEM] * (chips // 2),
    )(own_two, sibling_two)
    second = [
        send(messages_two[n], quarter=1, grp=lambda g, n=n: g ^ (2 * (2 * n + (g & 1))))
        for n in range(chips // 2)
    ]
    diagonal = []
    for first in (0, chips // 2):
        packed = call(
            pack,
            out_shape=f32(chips // 2, 2, part, columns),
            in_specs=[VMEM] * (chips // 2),
            out_specs=VMEM,
        )(*straight[first : first + chips // 2])
        diagonal.append(send(packed, quarter=1))
    other_second = call(
        pack_other,
        out_shape=f32(chips // 2, 2, part, columns),
        in_specs=[VMEM] * (chips // 2),
        out_specs=VMEM,
    )(*second)
    sibling_second = send(other_second, grp=lambda g: g ^ 1)
    factors = call(
        outer_factors,
        out_shape=f32(left_one.shape[0], 2 * rank),
        in_specs=[VMEM] * 4,
        out_specs=VMEM,
    )(left_one, middle_one, left_two, middle_two)
    return call(
        functools.partial(combine, chips),
        out_shape=f32(left_one.shape[0], columns),
        in_specs=[VMEM] * (4 + chips + chips // 2),
        out_specs=VMEM,
        scratch_shapes=[pltpu.VMEM((2 * rank, columns), jnp.float32)],
    )(factors, *straight, *diagonal, *second, sibling_second)


def project_far(order_one, order_two, rhs, right_one, right_two, slots_one, slots_two):
    part = slots_one.shape[1]
    levels = ((order_one, right_one, slots_one), (order_two, right_two, slots_two))
    for order, right, slots in levels:
        coeffs = product(right[...], rhs[...], ((0,), (0,)))
        for p in range(order.shape[2]):
            slots[order[0, 0, p]] = coeffs[p * part : (p + 1) * part]


def far(mesh, rhs, left_one, left_two, middle_one, middle_two, right_one, right_two, order_one, order_two):
    groups = mesh.shape["grp"]
    rank, columns = right_one.shape[1], rhs.shape[1]
    slots = pl.pallas_call(
        project_far,
        out_shape=[f32(groups, rank // groups, columns)] * 2,
        in_specs=[SMEM, SMEM, VMEM, VMEM, VMEM],
        out_specs=[VMEM, VMEM],
        compiler_params=PARAMS,
    )(order_one, order_two, rhs, right_one, right_two)
    swap = [(0, 1), (1, 0)]
    first, second = (
        lax.all_to_all(value, "grp", 0, 0, tiled=True).reshape(rank, columns) for value in slots
    )
    first = lax.ppermute(first, "half", swap)
    first = first + lax.ppermute(first, "quarter", swap)
    second = lax.ppermute(second, "quarter", swap)
    dot = functools.partial(jnp.dot, precision=lax.Precision.HIGHEST)
    result = dot(left_one, dot(middle_one[0, 0], first))
    return result + dot(left_two, dot(middle_two[0, 0], second))


def solution(mesh):
    in_specs = (
        P(AXES, None),
        P(AXES, None),
        P(AXES, None),
        P("half", "grp", None, None),
        P(("half", "quarter"), "grp", None, None),
        P(AXES, None),
        P(AXES, None),
        P("half", "grp", None),
        P(("half", "quarter"), "grp", None),
    )
    groups = mesh.shape["grp"]
    direct = groups >= 4 and groups & (groups - 1) == 0 and groups // 2 <= MOST_CHIPS
    return jax.shard_map(
        functools.partial(near if direct else far, mesh),
        mesh=mesh,
        in_specs=in_specs,
        out_specs=P(AXES, None),
        check_vma=False,
    )
```

time: 32.5 us -> 29.2 us (0.90)
  starting transfers between devices: 21.7 us -> 15.8 us
  waiting for transfers between devices: 3.92 us -> 8.54 us
  local copies, waits for them, and re-layouts: 4.17 us -> 0.03 us
  Pallas kernels: 2.52 us -> 4.56 us
    ppermute x13 -> x11, starting transfers between devices: 21.7 us -> 15.8 us  [send(): return lax.ppermute(value, AXES, pairs)]
    ppermute x13 -> x11, waiting for transfers between devices: 3.92 us -> 8.54 us  [send(): return lax.ppermute(value, AXES, pairs)]
    unnamed x18 -> x8, local copies, waits for them, and re-layouts: 4.17 us -> 0.03 us
    pallas_call x4 -> x9, Pallas kernels: 2.52 us -> 4.56 us  [the longest x1 2.12 us: near(): call(project_one, out_shape=[f32(chips, part, columns), f32(chips, part,...]
  transfers between devices with their start and end apart: 13 -> 11, of which waited for: 6 -> 4; matrix products, arithmetic and copies ran while one was open for 0% -> 0% of each run, Pallas kernels for 1% -> 4%
where the time goes in v2:
time: 29.2 us; the launch traced here: 29.1 us
  starting transfers between devices  15.8 us (54%)
  waiting for transfers between devices  8.54 us (29%)
  Pallas kernels  4.56 us (16%)
    ppermute x11, starting transfers between devices, send(): return lax.ppermute(value, AXES, pairs)  15.8 us
    ppermute x11, waiting for transfers between devices, send(): return lax.ppermute(value, AXES, pairs)  8.54 us
    pallas_call x1, Pallas kernels, near(): call(project_one, out_shape=[f32(chips, part, columns), f32(chips, part,...  2.12 us
    pallas_call x1, Pallas kernels, near(): call(functools.partial(combine, chips), out_shape=f32(left_one.shape[0],...  1.24 us
    pallas_call x1, Pallas kernels, near(): call(project_two, out_shape=[f32(chips // 2, 2, part, columns)] * 2, in_s...  0.89 us
  transfers between devices with their start and end apart: 11, of which 4 were waited for; matrix products, arithmetic and copies ran while one was open for 0% of the time, Pallas kernels for 4%

profile of v2, /device:TPU:0, one launch (start us, length us, event | category | flops | bytes accessed | tf_op | source)
XLA Modules:
  0.0 29.1 jit_solution(8351332464501203967)
XLA Ops:
  0.0 2.1 %shard_map.92 = (f32[4,16,512]{2,1,0:T(8,128)S(1)}, f32[4,16,512]{2,1,0:T(8,128)S(1)}, f32[256,512]{1,0:T(8,128)S(1)}, f32[256,128]{1,0:T(8,128)S(1)}, s32[1,1,8]{2,1,0:T(1,128)S(1)}) custom-call(s32[1,1,8]{2,1,0:T(1,128)} %order_one.1, s32[1,1,8]{2,1,0:T(1,128)} %order_two.1, f32[256,512]{1,0:T(8,128)} %rhs.1, f32[256,128]{1,0:T(8,128)} %right_one.1, ...), custom_call_target="tpu_custom_call" | custom-call | tf_op jit(solution)/shard_map/pallas_call | solution.py:160
  2.1 0.5 %collective-permute-start = (f32[4,16,512]{2,1,0:T(8,128)S(1)}, f32[4,16,512]{2,1,0:T(8,128)S(1)}, u32[]{:S(2)}, u32[]{:S(2)}) collective-permute-start(f32[4,16,512]{2,1,0:T(8,128)S(1)} %get-tuple-element.19), channel_id=1, source_target_pairs={{0,1},{1,0},{2,3},{3,2},{4,5},{5,4},{6,7},{7,6},{8,9},{9,8},{10,11... | collective-permute-start | bytes 393224 | tf_op jit(solution)/shard_map/ppermute | solution.py:158
  2.6 0.9 %shard_map.96 = (f32[2,2,16,512]{3,2,1,0:T(8,128)S(1)}, f32[2,2,16,512]{3,2,1,0:T(8,128)S(1)}) custom-call(s32[1,1,8]{2,1,0:T(1,128)S(1)} %get-tuple-element.24.order, f32[256,512]{1,0:T(8,128)S(1)} %get-tuple-element.25.rhs, f32[256,128]{1,0:T(8,128)S(1)} %get-tuple-element.26.right), custom_call_target="tpu_custom_call" | custom-call | tf_op jit(solution)/shard_map/pallas_call | solution.py:179
  3.5 0.1 collective-permute-start.7
  3.7 0.0 collective-permute-done.sibling
  3.7 5.0 %collective-permute-start.3 = (f32[2,16,512]{2,1,0:T(8,128)S(1)}, f32[2,16,512]{2,1,0:T(8,128)S(1)}, u32[]{:S(2)}, u32[]{:S(2)}) collective-permute-start(f32[2,16,512]{2,1,0:T(8,128)S(1)} %get-tuple-element.22), channel_id=1, source_target_pairs={{0,20},{1,21},{2,22},{3,23},{4,16},{5,17},{6,18},{7,19},{8,28},{9,... | collective-permute-start | bytes 196616 | tf_op jit(solution)/shard_map/ppermute | solution.py:158
  8.7 0.0 collective-permute-done.7.sibling
  8.7 1.6 %collective-permute-start.8 = (f32[2,2,16,512]{3,2,1,0:T(8,128)S(1)}, f32[2,2,16,512]{3,2,1,0:T(8,128)S(1)}, u32[]{:S(2)}, u32[]{:S(2)}) collective-permute-start(f32[2,2,16,512]{3,2,1,0:T(8,128)S(1)} %get-tuple-element.29), channel_id=1, source_target_pairs={{0,8},{1,11},{2,10},{3,9},{4,12},{5,15},{6,14},{7,13},{8,0},{9,3},... | collective-permute-start | bytes 393224 | tf_op jit(solution)/shard_map/ppermute | solution.py:158
  10.3 0.3 collective-permute-start.9
  10.6 3.6 %collective-permute-start.4 = (f32[2,16,512]{2,1,0:T(8,128)S(1)}, f32[2,16,512]{2,1,0:T(8,128)S(1)}, u32[]{:S(2)}, u32[]{:S(2)}) collective-permute-start(f32[2,16,512]{2,1,0:T(8,128)S(1)} %get-tuple-element.23), channel_id=1, source_target_pairs={{0,22},{1,23},{2,20},{3,21},{4,18},{5,19},{6,16},{7,17},{8,30},{9,... | collective-permute-start | bytes 196616 | tf_op jit(solution)/shard_map/ppermute | solution.py:158
  14.2 1.5 %collective-permute-start.1 = (f32[2,16,512]{2,1,0:T(8,128)S(1)}, f32[2,16,512]{2,1,0:T(8,128)S(1)}, u32[]{:S(2)}, u32[]{:S(2)}) collective-permute-start(f32[2,16,512]{2,1,0:T(8,128)S(1)} %get-tuple-element.20), channel_id=1, source_target_pairs={{0,16},{1,17},{2,18},{3,19},{4,20},{5,21},{6,22},{7,23},{8,24},{9,... | collective-permute-start | bytes 196616 | tf_op jit(solution)/shard_map/ppermute | solution.py:158
  15.7 0.0 collective-permute-done.3.refs_0_.refs_2_
  15.7 0.0 collective-permute-start.2
  15.7 4.2 %collective-permute-done.4.refs_1_.refs_3_ = f32[2,16,512]{2,1,0:T(8,128)S(1)} collective-permute-done((f32[2,16,512]{2,1,0:T(8,128)S(1)}, f32[2,16,512]{2,1,0:T(8,128)S(1)}, u32[]{:S(2)}, u32[]{:S(2)}) %collective-permute-start.4) | collective-permute-done | bytes 65568 | tf_op jit(solution)/shard_map/ppermute | solution.py:158
  19.9 1.6 %collective-permute-start.6 = (f32[2,2,16,512]{3,2,1,0:T(8,128)S(1)}, f32[2,2,16,512]{3,2,1,0:T(8,128)S(1)}, u32[]{:S(2)}, u32[]{:S(2)}) collective-permute-start(f32[2,2,16,512]{3,2,1,0:T(8,128)S(1)} %shard_map.95), channel_id=1, source_target_pairs={{0,8},{1,9},{2,10},{3,11},{4,12},{5,13},{6,14},{7,15},{8,0},{9,1},... | collective-permute-start | bytes 393224 | tf_op jit(solution)/shard_map/ppermute | solution.py:158
  21.5 0.0 collective-permute-done.1.refs_0_
  21.5 0.5 %collective-permute-done.2.refs_1_ = f32[2,16,512]{2,1,0:T(8,128)S(1)} collective-permute-done((f32[2,16,512]{2,1,0:T(8,128)S(1)}, f32[2,16,512]{2,1,0:T(8,128)S(1)}, u32[]{:S(2)}, u32[]{:S(2)}) %collective-permute-start.2) | collective-permute-done | bytes 65568 | tf_op jit(solution)/shard_map/ppermute | solution.py:158
  22.1 0.0 copy-start
  22.1 0.0 copy-start.1
  22.1 0.0 copy-start.2
  22.1 0.0 copy-start.3
  22.1 1.6 %collective-permute-start.5 = (f32[2,2,16,512]{3,2,1,0:T(8,128)S(1)}, f32[2,2,16,512]{3,2,1,0:T(8,128)S(1)}, u32[]{:S(2)}, u32[]{:S(2)}) collective-permute-start(f32[2,2,16,512]{3,2,1,0:T(8,128)S(1)} %shard_map.94), channel_id=1, source_target_pairs={{0,8},{1,9},{2,10},{3,11},{4,12},{5,13},{6,14},{7,15},{8,0},{9,1},... | collective-permute-start | bytes 393224 | tf_op jit(solution)/shard_map/ppermute | solution.py:158
  23.7 0.0 collective-permute-done.8.refs_0_.refs_6_
  23.7 0.0 collective-permute-done.9.refs_1_.refs_7_
  23.7 0.1 collective-permute-start.10
  23.8 0.0 copy-done
  23.8 0.0 copy-done.1
  23.8 0.0 copy-done.2
  23.8 0.0 copy-done.3
  23.8 0.2 shard_map.91.factors
  24.1 1.5 %collective-permute-done.6.refs_5_ = f32[2,2,16,512]{3,2,1,0:T(8,128)S(1)} collective-permute-done((f32[2,2,16,512]{3,2,1,0:T(8,128)S(1)}, f32[2,2,16,512]{3,2,1,0:T(8,128)S(1)}, u32[]{:S(2)}, u32[]{:S(2)}) %collective-permute-start.6) | collective-permute-done | bytes 131104 | tf_op jit(solution)/shard_map/ppermute | solution.py:158
  25.6 2.2 %collective-permute-done.5.refs_4_ = f32[2,2,16,512]{3,2,1,0:T(8,128)S(1)} collective-permute-done((f32[2,2,16,512]{3,2,1,0:T(8,128)S(1)}, f32[2,2,16,512]{3,2,1,0:T(8,128)S(1)}, u32[]{:S(2)}, u32[]{:S(2)}) %collective-permute-start.5) | collective-permute-done | bytes 131104 | tf_op jit(solution)/shard_map/ppermute | solution.py:158
  27.8 0.0 collective-permute-done.10.refs_8_
  27.9 1.2 %shard_map.99 = f32[256,512]{1,0:T(8,128)} custom-call(f32[256,256]{1,0:T(8,128)S(1)} %shard_map.91.factors, f32[2,16,512]{2,1,0:T(8,128)S(1)} %collective-permute-done.1.refs_0_, f32[2,16,512]{2,1,0:T(8,128)S(1)} %collective-permute-done.2.refs_1_, f32[2,16,512]{2,1,0:T(8,128)S(1)} %collective-permute-done.3.refs_0_.refs_2_, ...), custom_call_target="tpu_custom_call" | custom-call | tf_op jit(solution)/shard_map/pallas_call | solution.py:226
  (5 shorter events, 0.1 us)
Async XLA Ops:
  2.1 1.5 %collective-permute-start = (f32[4,16,512]{2,1,0:T(8,128)S(1)}, f32[4,16,512]{2,1,0:T(8,128)S(1)}, u32[]{:S(2)}, u32[]{:S(2)}) collective-permute-start(f32[4,16,512]{2,1,0:T(8,128)S(1)} %get-tuple-element.19), channel_id=1, source_target_pairs={{0,1},{1,0},{2,3},{3,2},{4,5},{5,4},{6,7},{7,6},{8,9},{9,8},{10,11... | collective-permute-start | bytes 393224 | tf_op jit(solution)/shard_map/ppermute | solution.py:158
  3.5 5.2 %collective-permute-start.7 = (f32[2,2,16,512]{3,2,1,0:T(8,128)S(1)}, f32[2,2,16,512]{3,2,1,0:T(8,128)S(1)}, u32[]{:S(2)}, u32[]{:S(2)}) collective-permute-start(f32[2,2,16,512]{3,2,1,0:T(8,128)S(1)} %get-tuple-element.28), channel_id=1, source_target_pairs={{0,1},{1,0},{2,3},{3,2},{4,5},{5,4},{6,7},{7,6},{8,9},{9,8},{10,11... | collective-permute-start | bytes 393224 | tf_op jit(solution)/shard_map/ppermute | solution.py:158
  3.7 12.0 %collective-permute-start.3 = (f32[2,16,512]{2,1,0:T(8,128)S(1)}, f32[2,16,512]{2,1,0:T(8,128)S(1)}, u32[]{:S(2)}, u32[]{:S(2)}) collective-permute-start(f32[2,16,512]{2,1,0:T(8,128)S(1)} %get-tuple-element.22), channel_id=1, source_target_pairs={{0,20},{1,21},{2,22},{3,23},{4,16},{5,17},{6,18},{7,19},{8,28},{9,... | collective-permute-start | bytes 196616 | tf_op jit(solution)/shard_map/ppermute | solution.py:158
  8.7 15.0 %collective-permute-start.8 = (f32[2,2,16,512]{3,2,1,0:T(8,128)S(1)}, f32[2,2,16,512]{3,2,1,0:T(8,128)S(1)}, u32[]{:S(2)}, u32[]{:S(2)}) collective-permute-start(f32[2,2,16,512]{3,2,1,0:T(8,128)S(1)} %get-tuple-element.29), channel_id=1, source_target_pairs={{0,8},{1,11},{2,10},{3,9},{4,12},{5,15},{6,14},{7,13},{8,0},{9,3},... | collective-permute-start | bytes 393224 | tf_op jit(solution)/shard_map/ppermute | solution.py:158
  10.3 13.4 %collective-permute-start.9 = (f32[2,2,16,512]{3,2,1,0:T(8,128)S(1)}, f32[2,2,16,512]{3,2,1,0:T(8,128)S(1)}, u32[]{:S(2)}, u32[]{:S(2)}) collective-permute-start(f32[2,2,16,512]{3,2,1,0:T(8,128)S(1)} %get-tuple-element.30), channel_id=1, source_target_pairs={{0,12},{1,15},{2,14},{3,13},{4,8},{5,11},{6,10},{7,9},{8,4},{9,7},... | collective-permute-start | bytes 393224 | tf_op jit(solution)/shard_map/ppermute | solution.py:158
  10.6 9.3 %collective-permute-start.4 = (f32[2,16,512]{2,1,0:T(8,128)S(1)}, f32[2,16,512]{2,1,0:T(8,128)S(1)}, u32[]{:S(2)}, u32[]{:S(2)}) collective-permute-start(f32[2,16,512]{2,1,0:T(8,128)S(1)} %get-tuple-element.23), channel_id=1, source_target_pairs={{0,22},{1,23},{2,20},{3,21},{4,18},{5,19},{6,16},{7,17},{8,30},{9,... | collective-permute-start | bytes 196616 | tf_op jit(solution)/shard_map/ppermute | solution.py:158
  14.2 7.3 %collective-permute-start.1 = (f32[2,16,512]{2,1,0:T(8,128)S(1)}, f32[2,16,512]{2,1,0:T(8,128)S(1)}, u32[]{:S(2)}, u32[]{:S(2)}) collective-permute-start(f32[2,16,512]{2,1,0:T(8,128)S(1)} %get-tuple-element.20), channel_id=1, source_target_pairs={{0,16},{1,17},{2,18},{3,19},{4,20},{5,21},{6,22},{7,23},{8,24},{9,... | collective-permute-start | bytes 196616 | tf_op jit(solution)/shard_map/ppermute | solution.py:158
  15.7 6.4 %collective-permute-start.2 = (f32[2,16,512]{2,1,0:T(8,128)S(1)}, f32[2,16,512]{2,1,0:T(8,128)S(1)}, u32[]{:S(2)}, u32[]{:S(2)}) collective-permute-start(f32[2,16,512]{2,1,0:T(8,128)S(1)} %get-tuple-element.21), channel_id=1, source_target_pairs={{0,18},{1,19},{2,16},{3,17},{4,22},{5,23},{6,20},{7,21},{8,26},{9,... | collective-permute-start | bytes 196616 | tf_op jit(solution)/shard_map/ppermute | solution.py:158
  19.9 5.7 %collective-permute-start.6 = (f32[2,2,16,512]{3,2,1,0:T(8,128)S(1)}, f32[2,2,16,512]{3,2,1,0:T(8,128)S(1)}, u32[]{:S(2)}, u32[]{:S(2)}) collective-permute-start(f32[2,2,16,512]{3,2,1,0:T(8,128)S(1)} %shard_map.95), channel_id=1, source_target_pairs={{0,8},{1,9},{2,10},{3,11},{4,12},{5,13},{6,14},{7,15},{8,0},{9,1},... | collective-permute-start | bytes 393224 | tf_op jit(solution)/shard_map/ppermute | solution.py:158
  22.1 1.7 %copy-start = (f32[256,128]{1,0:T(8,128)S(1)}, f32[256,128]{1,0:T(8,128)}, u32[]{:S(2)}) copy-start(f32[256,128]{1,0:T(8,128)} %left_one.1) | copy-start | bytes 393220
  22.1 1.7 %copy-start.1 = (f32[256,128]{1,0:T(8,128)S(1)}, f32[256,128]{1,0:T(8,128)}, u32[]{:S(2)}) copy-start(f32[256,128]{1,0:T(8,128)} %left_two.1) | copy-start | bytes 393220
  22.1 1.7 %copy-start.2 = (f32[1,1,128,128]{3,2,1,0:T(8,128)S(1)}, f32[1,1,128,128]{3,2,1,0:T(8,128)}, u32[]{:S(2)}) copy-start(f32[1,1,128,128]{3,2,1,0:T(8,128)} %middle_one.1) | copy-start | bytes 196612
  22.1 1.7 %copy-start.3 = (f32[1,1,128,128]{3,2,1,0:T(8,128)S(1)}, f32[1,1,128,128]{3,2,1,0:T(8,128)}, u32[]{:S(2)}) copy-start(f32[1,1,128,128]{3,2,1,0:T(8,128)} %middle_two.1) | copy-start | bytes 196612
  22.1 5.7 %collective-permute-start.5 = (f32[2,2,16,512]{3,2,1,0:T(8,128)S(1)}, f32[2,2,16,512]{3,2,1,0:T(8,128)S(1)}, u32[]{:S(2)}, u32[]{:S(2)}) collective-permute-start(f32[2,2,16,512]{3,2,1,0:T(8,128)S(1)} %shard_map.94), channel_id=1, source_target_pairs={{0,8},{1,9},{2,10},{3,11},{4,12},{5,13},{6,14},{7,15},{8,0},{9,1},... | collective-permute-start | bytes 393224 | tf_op jit(solution)/shard_map/ppermute | solution.py:158
  23.7 4.1 %collective-permute-start.10 = (f32[2,2,16,512]{3,2,1,0:T(8,128)S(1)}, f32[2,2,16,512]{3,2,1,0:T(8,128)S(1)}, u32[]{:S(2)}, u32[]{:S(2)}) collective-permute-start(f32[2,2,16,512]{3,2,1,0:T(8,128)S(1)} %shard_map.98), channel_id=1, source_target_pairs={{0,1},{1,0},{2,3},{3,2},{4,5},{5,4},{6,7},{7,6},{8,9},{9,8},{10,11... | collective-permute-start | bytes 393224 | tf_op jit(solution)/shard_map/ppermute | solution.py:158

commit v3 on v1

v3 whole, which is shorter than its diff:
```python
import functools

import jax
import jax.numpy as jnp
from jax import lax
from jax.experimental import pallas as pl
from jax.experimental.pallas import tpu as pltpu
from jax.sharding import PartitionSpec as P

AXES = ("half", "quarter", "grp")
MOST_CHIPS = 8
COST = 10**10
PARAMS = pltpu.CompilerParams(vmem_limit_bytes=16 * 2**20)
VMEM = pl.BlockSpec(memory_space=pltpu.VMEM)
ANY = pl.BlockSpec(memory_space=pl.ANY)
HBM = pl.BlockSpec(memory_space=pltpu.HBM)
SMEM = pl.BlockSpec(memory_space=pltpu.SMEM)


def f32(*shape):
    return jax.ShapeDtypeStruct(shape, jnp.float32)


def in_hbm(value):
    return pltpu.with_memory_space_constraint(value, pltpu.HBM)


def split(value):
    high = value.astype(jnp.bfloat16)
    low = (value - high.astype(jnp.float32)).astype(jnp.bfloat16)
    return high, low


def product(left, right, dims=((1,), (0,))):
    dot = functools.partial(
        lax.dot_general,
        dimension_numbers=(dims, ((), ())),
        preferred_element_type=jnp.float32,
    )
    (lh, ll), (rh, rl) = split(left), split(right)
    return dot(lh, rh) + (dot(lh, rl) + dot(ll, rh))


def project(
    order_one, order_two, rhs, right_one, right_two,
    kept_one, swapped_one, across_one, diagonal_one, kept_two, swapped_two,
    values, rights, slots_one, slots_two, orders, sems,
):
    rank = right_one.shape[1]
    pairs = (
        (right_one, rights.at[:, :rank]),
        (right_two, rights.at[:, rank:]),
        (rhs, values),
        (order_one, orders.at[0]),
        (order_two, orders.at[1]),
    )
    copies = [pltpu.make_async_copy(*pair, sems.at[n]) for n, pair in enumerate(pairs)]
    for copy in copies:
        copy.start()
    me = lax.axis_index("grp")
    quarter = lax.axis_index("quarter")
    for copy in copies:
        copy.wait()
    coeffs = product(rights[...], values[...], ((0,), (0,)))
    part = kept_one.shape[1]
    for p in range(rank // part):
        first, second = (coeffs[n * rank + p * part : n * rank + (p + 1) * part] for n in range(2))
        apart = orders[0, 0, 0, p] ^ me
        slots_one[((apart >> 1) ^ quarter) & 1, apart & 1, apart >> 2] = first
        receiver = orders[1, 0, 0, p]
        apart = (receiver >> 1) ^ (me >> 1)
        slots_two[(apart ^ me) & 1, apart >> 1, receiver & 1] = second
    kept_one[...] = slots_one[0, 0]
    swapped_one[...] = slots_one[0, 1]
    across_one[...] = slots_one[1, 0]
    diagonal_one[...] = slots_one[1, 1]
    kept_two[...] = slots_two[0]
    swapped_two[...] = slots_two[1]


def add_up(kept, swapped, across, diagonal, *messages):
    for n, message in enumerate(messages):
        message[0] = kept[n] + across[n]
        message[1] = swapped[n] + diagonal[n]


def pair_up(kept, swapped, *messages):
    for n, message in enumerate(messages):
        message[0] = kept[n]
        message[1] = swapped[n]


def pack_other(*refs):
    out = refs[-1]
    there = 1 - (lax.axis_index("grp") & 1)
    for n, ref in enumerate(refs[:-1]):
        out[n] = ref[:, there]


def outer_factors(left_one, middle_one, left_two, middle_two, factors):
    rank = left_one.shape[1]
    factors[:, :rank] = product(left_one[...], middle_one[0, 0])
    factors[:, rank:] = product(left_two[...], middle_two[0, 0])


def put(stacked, apart, rows):
    row = pl.multiple_of((lax.axis_index("grp") ^ apart) * rows.shape[0], rows.shape[0])
    stacked[pl.ds(row, rows.shape[0])] = rows


def regroup_one(*refs):
    stacked = refs[-1]
    half = (len(refs) - 1) // 2
    quarter = lax.axis_index("quarter")
    for n in range(half):
        for other in range(2):
            put(stacked, 4 * n + 2 * quarter + other, refs[n][other])
            put(stacked, 4 * n + 2 * (1 - quarter) + other, refs[half + n][other])


def combine(factors, first, other_second, *refs):
    second, (out, stacked) = refs[:-2], refs[-2:]
    core = lax.axis_index("grp") & 1
    for n in range(len(second)):
        for other in range(2):
            put(stacked, 4 * n + 2 * core + other, second[n][other, core])
            put(stacked, 4 * n + 2 * (1 - core) + 1 - other, other_second[n, other])
    rank = first.shape[0]
    out[...] = product(factors[:, :rank], first[...]) + product(factors[:, rank:], stacked[...])


def near(mesh, rhs, left_one, left_two, middle_one, middle_two, right_one, right_two, order_one, order_two):
    groups = mesh.shape["grp"]
    chips = groups // 2
    half = chips // 2
    rank, columns = right_one.shape[1], rhs.shape[1]
    part = rank // groups

    def call(kernel, out_shape, *operands, after=(), cost=None, scratch=()):
        taken = len(operands)

        def body(*refs):
            kernel(*refs[:taken], *refs[taken + len(after) :])

        return pl.pallas_call(
            body,
            out_shape=out_shape,
            in_specs=[HBM if kernel is project else VMEM] * taken + [ANY] * len(after),
            out_specs=jax.tree.map(lambda _: VMEM, out_shape),
            scratch_shapes=scratch,
            compiler_params=PARAMS,
            cost_estimate=cost and pl.CostEstimate(flops=cost, bytes_accessed=cost // 100, transcendentals=0),
        )(*operands, *after)

    def send(value, to):
        sizes = [mesh.shape[axis] for axis in AXES]
        pairs = []
        for h in range(sizes[0]):
            for q in range(sizes[1]):
                for g in range(sizes[2]):
                    a, b, c = to(h, q, g)
                    source = (h * sizes[1] + q) * sizes[2] + g
                    pairs.append((source, (a * sizes[1] + b) * sizes[2] + c))
        return lax.ppermute(value, AXES, pairs)

    def swap_cores(value):
        return send(value, lambda h, q, g: (h, q, g ^ 1))

    def swap_quarters(value):
        return send(value, lambda h, q, g: (h, 1 - q, g))

    kept_one, swapped_one, across_one, diagonal_one, kept_two, swapped_two = call(
        project,
        [f32(half, part, columns)] * 4 + [f32(half, 2, part, columns)] * 2,
        *(in_hbm(value) for value in (order_one, order_two, rhs, right_one, right_two)),
        scratch=[
            pltpu.VMEM(rhs.shape, jnp.float32),
            pltpu.VMEM((right_one.shape[0], 2 * rank), jnp.float32),
            pltpu.VMEM((2, 2, half, part, columns), jnp.float32),
            pltpu.VMEM((2, half, 2, part, columns), jnp.float32),
            pltpu.SMEM((2, *order_one.shape), jnp.int32),
            pltpu.SemaphoreType.DMA((5,)),
        ],
    )
    across_one = swap_quarters(across_one)
    diagonal_one = send(diagonal_one, lambda h, q, g: (h, 1 - q, g ^ 1))
    swapped_two = swap_cores(swapped_two)
    swapped_one = swap_cores(swapped_one)
    messages_two = call(pair_up, [f32(2, 2, part, columns)] * half, kept_two, swapped_two, after=(swapped_one,))
    second = [
        send(messages_two[n], lambda h, q, g, n=n: (h, 1 - q, g ^ (2 * (2 * n + (g & 1)))))
        for n in range(half)
    ]
    messages_one = call(
        add_up, [f32(2, part, columns)] * half, kept_one, swapped_one, across_one, diagonal_one, after=(messages_two[0],), cost=COST
    )
    first = [
        send(messages_one[n], lambda h, q, g, n=n: (1 - h, q, g ^ (2 * (2 * n + q))))
        for n in range(half)
    ]
    other_first = [swap_quarters(value) for value in first]
    other_second = swap_cores(call(pack_other, f32(half, 2, part, columns), *second))
    factors = call(
        outer_factors, f32(left_one.shape[0], 2 * rank), left_one, middle_one, left_two, middle_two
    )
    stacked = call(regroup_one, f32(rank, columns), *first, *other_first, cost=COST)
    return call(
        combine,
        f32(left_one.shape[0], columns),
        *(factors, stacked, other_second, *second),
        scratch=[pltpu.VMEM((rank, columns), jnp.float32)],
    )


def project_far(order_one, order_two, rhs, right_one, right_two, slots_one, slots_two):
    part = slots_one.shape[1]
    levels = ((order_one, right_one, slots_one), (order_two, right_two, slots_two))
    for order, right, slots in levels:
        coeffs = product(right[...], rhs[...], ((0,), (0,)))
        for p in range(order.shape[2]):
            slots[order[0, 0, p]] = coeffs[p * part : (p + 1) * part]


def far(mesh, rhs, left_one, left_two, middle_one, middle_two, right_one, right_two, order_one, order_two):
    groups = mesh.shape["grp"]
    rank, columns = right_one.shape[1], rhs.shape[1]
    slots = pl.pallas_call(
        project_far,
        out_shape=[f32(groups, rank // groups, columns)] * 2,
        in_specs=[SMEM, SMEM, VMEM, VMEM, VMEM],
        out_specs=[VMEM, VMEM],
        compiler_params=PARAMS,
    )(order_one, order_two, rhs, right_one, right_two)
    swap = [(0, 1), (1, 0)]
    first, second = (
        lax.all_to_all(value, "grp", 0, 0, tiled=True).reshape(rank, columns) for value in slots
    )
    first = lax.ppermute(first, "half", swap)
    first = first + lax.ppermute(first, "quarter", swap)
    second = lax.ppermute(second, "quarter", swap)
    dot = functools.partial(jnp.dot, precision=lax.Precision.HIGHEST)
    result = dot(left_one, dot(middle_one[0, 0], first))
    return result + dot(left_two, dot(middle_two[0, 0], second))


def solution(mesh):
    in_specs = (
        P(AXES, None),
        P(AXES, None),
        P(AXES, None),
        P("half", "grp", None, None),
        P(("half", "quarter"), "grp", None, None),
        P(AXES, None),
        P(AXES, None),
        P("half", "grp", None),
        P(("half", "quarter"), "grp", None),
    )
    groups = mesh.shape["grp"]
    direct = groups >= 4 and groups & (groups - 1) == 0 and groups // 2 <= MOST_CHIPS
    return jax.shard_map(
        functools.partial(near if direct else far, mesh),
        mesh=mesh,
        in_specs=in_specs,
        out_specs=P(AXES, None),
        check_vma=False,
    )
```

time: 32.5 us -> 25.7 us (0.79)
  starting transfers between devices: 21.7 us -> 17 us
  local copies, waits for them, and re-layouts: 4.17 us -> 0.01 us
  waiting for transfers between devices: 3.92 us -> 5.02 us
  Pallas kernels: 2.52 us -> 3.35 us
    ppermute x13 -> x11, starting transfers between devices: 21.7 us -> 17 us  [send(): return lax.ppermute(value, AXES, pairs)]
    unnamed x18 -> x8, local copies, waits for them, and re-layouts: 4.17 us -> 0.01 us
    ppermute x13 -> x11, waiting for transfers between devices: 3.92 us -> 5.02 us  [send(): return lax.ppermute(value, AXES, pairs)]
    pallas_call x4 -> x7, Pallas kernels: 2.52 us -> 3.35 us  [call(): pl.pallas_call(body, out_shape=out_shape, in_specs=[HBM if kernel is proj...]
  transfers between devices with their start and end apart: 13 -> 11, of which waited for: 6 -> 3; matrix products, arithmetic and copies ran while one was open for 0% -> 0% of each run, Pallas kernels for 1% -> 1%
where the time goes in v3:
time: 25.7 us; the launch traced here: 25.5 us
  starting transfers between devices  17 us (66%)
  waiting for transfers between devices  5.02 us (20%)
  Pallas kernels  3.35 us (13%)
    ppermute x11, starting transfers between devices, send(): return lax.ppermute(value, AXES, pairs)  17 us
    ppermute x11, waiting for transfers between devices, send(): return lax.ppermute(value, AXES, pairs)  5.02 us
    pallas_call x7, Pallas kernels, call(): pl.pallas_call(body, out_shape=out_shape, in_specs=[HBM if kernel is proj...  3.35 us
  transfers between devices with their start and end apart: 11, of which 3 were waited for; matrix products, arithmetic and copies ran while one was open for 0% of the time, Pallas kernels for 1%

profile of v3, /device:TPU:0, one launch (start us, length us, event | category | flops | bytes accessed | tf_op | source)
XLA Modules:
  0.0 25.5 jit_solution(7145919491890247042)
XLA Ops:
  0.0 1.7 %shard_map.92 = (f32[2,16,512]{2,1,0:T(8,128)S(1)}, f32[2,16,512]{2,1,0:T(8,128)S(1)}, f32[2,16,512]{2,1,0:T(8,128)S(1)}, f32[2,16,512]{2,1,0:T(8,128)S(1)}, f32...) custom-call(s32[1,1,8]{2,1,0:T(1,128)} %refs_0_.3, s32[1,1,8]{2,1,0:T(1,128)} %refs_1_.3, f32[256,512]{1,0:T(8,128)} %refs_2_.3, ...), custom_call_target="tpu_custom_call" | custom-call | tf_op jit(solution)/shard_map/pallas_call | solution.py:145
  1.7 0.5 %collective-permute-start.3 = (f32[2,2,16,512]{3,2,1,0:T(8,128)S(1)}, f32[2,2,16,512]{3,2,1,0:T(8,128)S(1)}, u32[]{:S(2)}, u32[]{:S(2)}) collective-permute-start(f32[2,2,16,512]{3,2,1,0:T(8,128)S(1)} %get-tuple-element.20), channel_id=1, source_target_pairs={{0,1},{1,0},{2,3},{3,2},{4,5},{5,4},{6,7},{7,6},{8,9},{9,8},{10,11... | collective-permute-start | bytes 393224 | tf_op jit(solution)/shard_map/ppermute | solution.py:164
  2.2 0.1 collective-permute-start
  2.3 3.0 %collective-permute-start.1 = (f32[2,16,512]{2,1,0:T(8,128)S(1)}, f32[2,16,512]{2,1,0:T(8,128)S(1)}, u32[]{:S(2)}, u32[]{:S(2)}) collective-permute-start(f32[2,16,512]{2,1,0:T(8,128)S(1)} %get-tuple-element.17), channel_id=1, source_target_pairs={{0,8},{1,9},{2,10},{3,11},{4,12},{5,13},{6,14},{7,15},{8,0},{9,1},... | collective-permute-start | bytes 196616 | tf_op jit(solution)/shard_map/ppermute | solution.py:164
  5.2 0.0 collective-permute-start.2
  5.2 0.0 collective-permute-done.refs_2_.refs_1_
  5.2 0.0 collective-permute-done.3.refs_1_
  5.3 3.5 %collective-permute-start.9 = (f32[2,2,16,512]{3,2,1,0:T(8,128)S(1)}, f32[2,2,16,512]{3,2,1,0:T(8,128)S(1)}, u32[]{:S(2)}, u32[]{:S(2)}) collective-permute-start(f32[2,2,16,512]{3,2,1,0:T(8,128)S(1)} %get-tuple-element.24), channel_id=1, source_target_pairs={{0,12},{1,15},{2,14},{3,13},{4,8},{5,11},{6,10},{7,9},{8,4},{9,7},... | collective-permute-start | bytes 393224 | tf_op jit(solution)/shard_map/ppermute | solution.py:164
  8.8 0.6 %collective-permute-start.8 = (f32[2,2,16,512]{3,2,1,0:T(8,128)S(1)}, f32[2,2,16,512]{3,2,1,0:T(8,128)S(1)}, u32[]{:S(2)}, u32[]{:S(2)}) collective-permute-start(f32[2,2,16,512]{3,2,1,0:T(8,128)S(1)} %get-tuple-element.21.refs_4_), channel_id=1, source_target_pairs={{0,8},{1,11},{2,10},{3,9},{4,12},{5,15},{6,14},{7,13},{8,0},{9,3},... | collective-permute-start | bytes 393224 | tf_op jit(solution)/shard_map/ppermute | solution.py:164
  9.4 0.0 collective-permute-done.1.refs_2_
  9.4 0.2 collective-permute-done.2.refs_3_
  9.6 0.0 copy-start
  9.6 0.0 copy-start.1
  9.6 0.0 copy-start.2
  9.6 0.0 copy-start.3
  9.6 1.6 %collective-permute-start.4 = (f32[2,16,512]{2,1,0:T(8,128)S(1)}, f32[2,16,512]{2,1,0:T(8,128)S(1)}, u32[]{:S(2)}, u32[]{:S(2)}) collective-permute-start(f32[2,16,512]{2,1,0:T(8,128)S(1)} %get-tuple-element.22), channel_id=1, source_target_pairs={{0,16},{1,17},{2,18},{3,19},{4,20},{5,21},{6,22},{7,23},{8,26},{9,... | collective-permute-start | bytes 196616 | tf_op jit(solution)/shard_map/ppermute | solution.py:164
  11.2 4.6 %collective-permute-start.5 = (f32[2,16,512]{2,1,0:T(8,128)S(1)}, f32[2,16,512]{2,1,0:T(8,128)S(1)}, u32[]{:S(2)}, u32[]{:S(2)}) collective-permute-start(f32[2,16,512]{2,1,0:T(8,128)S(1)} %get-tuple-element.23), channel_id=1, source_target_pairs={{0,20},{1,21},{2,22},{3,23},{4,16},{5,17},{6,18},{7,19},{8,30},{9,... | collective-permute-start | bytes 196616 | tf_op jit(solution)/shard_map/ppermute | solution.py:164
  15.8 0.0 collective-permute-done.4.refs_0_
  15.8 2.0 %collective-permute-start.6 = (f32[2,16,512]{2,1,0:T(8,128)S(1)}, f32[2,16,512]{2,1,0:T(8,128)S(1)}, u32[]{:S(2)}, u32[]{:S(2)}) collective-permute-start(f32[2,16,512]{2,1,0:T(8,128)S(1)} %collective-permute-done.4.refs_0_), channel_id=1, source_target_pairs={{0,8},{1,9},{2,10},{3,11},{4,12},{5,13},{6,14},{7,15},{8,0},{9,1},... | collective-permute-start | bytes 196616 | tf_op jit(solution)/shard_map/ppermute | solution.py:164
  17.9 2.0 %collective-permute-done.5.refs_1_ = f32[2,16,512]{2,1,0:T(8,128)S(1)} collective-permute-done((f32[2,16,512]{2,1,0:T(8,128)S(1)}, f32[2,16,512]{2,1,0:T(8,128)S(1)}, u32[]{:S(2)}, u32[]{:S(2)}) %collective-permute-start.5) | collective-permute-done | bytes 65568 | tf_op jit(solution)/shard_map/ppermute | solution.py:164
  19.8 1.1 %collective-permute-start.7 = (f32[2,16,512]{2,1,0:T(8,128)S(1)}, f32[2,16,512]{2,1,0:T(8,128)S(1)}, u32[]{:S(2)}, u32[]{:S(2)}) collective-permute-start(f32[2,16,512]{2,1,0:T(8,128)S(1)} %collective-permute-done.5.refs_1_), channel_id=1, source_target_pairs={{0,8},{1,9},{2,10},{3,11},{4,12},{5,13},{6,14},{7,15},{8,0},{9,1},... | collective-permute-start | bytes 196616 | tf_op jit(solution)/shard_map/ppermute | solution.py:164
  20.9 0.0 copy-done
  20.9 0.0 copy-done.1
  20.9 0.0 copy-done.2
  20.9 0.0 copy-done.3
  20.9 0.2 shard_map.91.refs_0_
  21.2 0.0 collective-permute-done.9.refs_1_.refs_4_
  21.2 0.0 collective-permute-done.8.refs_0_.refs_3_
  21.2 0.1 collective-permute-start.10
  21.3 0.0 collective-permute-done.6.refs_2_
  21.3 2.8 %collective-permute-done.7.refs_3_ = f32[2,16,512]{2,1,0:T(8,128)S(1)} collective-permute-done((f32[2,16,512]{2,1,0:T(8,128)S(1)}, f32[2,16,512]{2,1,0:T(8,128)S(1)}, u32[]{:S(2)}, u32[]{:S(2)}) %collective-permute-start.7) | collective-permute-done | bytes 65568 | tf_op jit(solution)/shard_map/ppermute | solution.py:164
  24.2 0.0 collective-permute-done.10.refs_2_
  24.2 1.4 %shard_map.97 = f32[256,512]{1,0:T(8,128)} custom-call(f32[256,256]{1,0:T(8,128)S(1)} %shard_map.91.refs_0_, f32[128,512]{1,0:T(8,128)S(1)} %shard_map.95.refs_1_, f32[2,2,16,512]{3,2,1,0:T(8,128)S(1)} %collective-permute-done.10.refs_2_, f32[2,2,16,512]{3,2,1,0:T(8,128)S(1)} %collective-permute-done.8.refs_0_.refs_3_, ...), custom_call_target="tpu_custom_call" | custom-call | tf_op jit(solution)/shard_map/pallas_call | solution.py:145
  (4 shorter events, 0.1 us)
Async XLA Ops:
  1.7 3.6 %collective-permute-start.3 = (f32[2,2,16,512]{3,2,1,0:T(8,128)S(1)}, f32[2,2,16,512]{3,2,1,0:T(8,128)S(1)}, u32[]{:S(2)}, u32[]{:S(2)}) collective-permute-start(f32[2,2,16,512]{3,2,1,0:T(8,128)S(1)} %get-tuple-element.20), channel_id=1, source_target_pairs={{0,1},{1,0},{2,3},{3,2},{4,5},{5,4},{6,7},{7,6},{8,9},{9,8},{10,11... | collective-permute-start | bytes 393224 | tf_op jit(solution)/shard_map/ppermute | solution.py:164
  2.2 3.0 %collective-permute-start = (f32[2,16,512]{2,1,0:T(8,128)S(1)}, f32[2,16,512]{2,1,0:T(8,128)S(1)}, u32[]{:S(2)}, u32[]{:S(2)}) collective-permute-start(f32[2,16,512]{2,1,0:T(8,128)S(1)} %get-tuple-element.16), channel_id=1, source_target_pairs={{0,1},{1,0},{2,3},{3,2},{4,5},{5,4},{6,7},{7,6},{8,9},{9,8},{10,11... | collective-permute-start | bytes 196616 | tf_op jit(solution)/shard_map/ppermute | solution.py:164
  2.3 7.1 %collective-permute-start.1 = (f32[2,16,512]{2,1,0:T(8,128)S(1)}, f32[2,16,512]{2,1,0:T(8,128)S(1)}, u32[]{:S(2)}, u32[]{:S(2)}) collective-permute-start(f32[2,16,512]{2,1,0:T(8,128)S(1)} %get-tuple-element.17), channel_id=1, source_target_pairs={{0,8},{1,9},{2,10},{3,11},{4,12},{5,13},{6,14},{7,15},{8,0},{9,1},... | collective-permute-start | bytes 196616 | tf_op jit(solution)/shard_map/ppermute | solution.py:164
  5.2 4.4 %collective-permute-start.2 = (f32[2,16,512]{2,1,0:T(8,128)S(1)}, f32[2,16,512]{2,1,0:T(8,128)S(1)}, u32[]{:S(2)}, u32[]{:S(2)}) collective-permute-start(f32[2,16,512]{2,1,0:T(8,128)S(1)} %get-tuple-element.18), channel_id=1, source_target_pairs={{0,9},{1,8},{2,11},{3,10},{4,13},{5,12},{6,15},{7,14},{8,1},{9,0},... | collective-permute-start | bytes 196616 | tf_op jit(solution)/shard_map/ppermute | solution.py:164
  5.3 15.9 %collective-permute-start.9 = (f32[2,2,16,512]{3,2,1,0:T(8,128)S(1)}, f32[2,2,16,512]{3,2,1,0:T(8,128)S(1)}, u32[]{:S(2)}, u32[]{:S(2)}) collective-permute-start(f32[2,2,16,512]{3,2,1,0:T(8,128)S(1)} %get-tuple-element.24), channel_id=1, source_target_pairs={{0,12},{1,15},{2,14},{3,13},{4,8},{5,11},{6,10},{7,9},{8,4},{9,7},... | collective-permute-start | bytes 393224 | tf_op jit(solution)/shard_map/ppermute | solution.py:164
  8.8 12.4 %collective-permute-start.8 = (f32[2,2,16,512]{3,2,1,0:T(8,128)S(1)}, f32[2,2,16,512]{3,2,1,0:T(8,128)S(1)}, u32[]{:S(2)}, u32[]{:S(2)}) collective-permute-start(f32[2,2,16,512]{3,2,1,0:T(8,128)S(1)} %get-tuple-element.21.refs_4_), channel_id=1, source_target_pairs={{0,8},{1,11},{2,10},{3,9},{4,12},{5,15},{6,14},{7,13},{8,0},{9,3},... | collective-permute-start | bytes 393224 | tf_op jit(solution)/shard_map/ppermute | solution.py:164
  9.6 11.3 %copy-start = (f32[256,128]{1,0:T(8,128)S(1)}, f32[256,128]{1,0:T(8,128)}, u32[]{:S(2)}) copy-start(f32[256,128]{1,0:T(8,128)} %refs_0_.2) | copy-start | bytes 393220
  9.6 11.3 %copy-start.1 = (f32[256,128]{1,0:T(8,128)S(1)}, f32[256,128]{1,0:T(8,128)}, u32[]{:S(2)}) copy-start(f32[256,128]{1,0:T(8,128)} %refs_2_.2) | copy-start | bytes 393220
  9.6 11.3 %copy-start.2 = (f32[1,1,128,128]{3,2,1,0:T(8,128)S(1)}, f32[1,1,128,128]{3,2,1,0:T(8,128)}, u32[]{:S(2)}) copy-start(f32[1,1,128,128]{3,2,1,0:T(8,128)} %refs_1_.2) | copy-start | bytes 196612
  9.6 11.3 %copy-start.3 = (f32[1,1,128,128]{3,2,1,0:T(8,128)S(1)}, f32[1,1,128,128]{3,2,1,0:T(8,128)}, u32[]{:S(2)}) copy-start(f32[1,1,128,128]{3,2,1,0:T(8,128)} %refs_3_.2) | copy-start | bytes 196612
  9.6 6.2 %collective-permute-start.4 = (f32[2,16,512]{2,1,0:T(8,128)S(1)}, f32[2,16,512]{2,1,0:T(8,128)S(1)}, u32[]{:S(2)}, u32[]{:S(2)}) collective-permute-start(f32[2,16,512]{2,1,0:T(8,128)S(1)} %get-tuple-element.22), channel_id=1, source_target_pairs={{0,16},{1,17},{2,18},{3,19},{4,20},{5,21},{6,22},{7,23},{8,26},{9,... | collective-permute-start | bytes 196616 | tf_op jit(solution)/shard_map/ppermute | solution.py:164
  11.2 8.7 %collective-permute-start.5 = (f32[2,16,512]{2,1,0:T(8,128)S(1)}, f32[2,16,512]{2,1,0:T(8,128)S(1)}, u32[]{:S(2)}, u32[]{:S(2)}) collective-permute-start(f32[2,16,512]{2,1,0:T(8,128)S(1)} %get-tuple-element.23), channel_id=1, source_target_pairs={{0,20},{1,21},{2,22},{3,23},{4,16},{5,17},{6,18},{7,19},{8,30},{9,... | collective-permute-start | bytes 196616 | tf_op jit(solution)/shard_map/ppermute | solution.py:164
  15.8 5.5 %collective-permute-start.6 = (f32[2,16,512]{2,1,0:T(8,128)S(1)}, f32[2,16,512]{2,1,0:T(8,128)S(1)}, u32[]{:S(2)}, u32[]{:S(2)}) collective-permute-start(f32[2,16,512]{2,1,0:T(8,128)S(1)} %collective-permute-done.4.refs_0_), channel_id=1, source_target_pairs={{0,8},{1,9},{2,10},{3,11},{4,12},{5,13},{6,14},{7,15},{8,0},{9,1},... | collective-permute-start | bytes 196616 | tf_op jit(solution)/shard_map/ppermute | solution.py:164
  19.8 4.3 %collective-permute-start.7 = (f32[2,16,512]{2,1,0:T(8,128)S(1)}, f32[2,16,512]{2,1,0:T(8,128)S(1)}, u32[]{:S(2)}, u32[]{:S(2)}) collective-permute-start(f32[2,16,512]{2,1,0:T(8,128)S(1)} %collective-permute-done.5.refs_1_), channel_id=1, source_target_pairs={{0,8},{1,9},{2,10},{3,11},{4,12},{5,13},{6,14},{7,15},{8,0},{9,1},... | collective-permute-start | bytes 196616 | tf_op jit(solution)/shard_map/ppermute | solution.py:164
  21.2 2.9 %collective-permute-start.10 = (f32[2,2,16,512]{3,2,1,0:T(8,128)S(1)}, f32[2,2,16,512]{3,2,1,0:T(8,128)S(1)}, u32[]{:S(2)}, u32[]{:S(2)}) collective-permute-start(f32[2,2,16,512]{3,2,1,0:T(8,128)S(1)} %shard_map.96), channel_id=1, source_target_pairs={{0,1},{1,0},{2,3},{3,2},{4,5},{5,4},{6,7},{7,6},{8,9},{9,8},{10,11... | collective-permute-start | bytes 393224 | tf_op jit(solution)/shard_map/ppermute | solution.py:164

commit v4 on v3

--- a/solution.py
+++ b/solution.py
@@ -62,17 +62,19 @@
     for copy in copies:
         copy.wait()
     coeffs = product(rights[...], values[...], ((0,), (0,)))
-    part = kept_one.shape[1]
+    part = slots_one.shape[4]
     for p in range(rank // part):
         first, second = (coeffs[n * rank + p * part : n * rank + (p + 1) * part] for n in range(2))
-        apart = orders[0, 0, 0, p] ^ me
-        slots_one[((apart >> 1) ^ quarter) & 1, apart & 1, apart >> 2] = first
+        receiver = orders[0, 0, 0, p]
+        apart = (receiver >> 1) ^ (me >> 1)
+        core = ((apart >> 1) ^ me) & 1
+        slots_one[core, (apart ^ quarter) & 1, apart >> 2, receiver & 1] = first
         receiver = orders[1, 0, 0, p]
         apart = (receiver >> 1) ^ (me >> 1)
         slots_two[(apart ^ me) & 1, apart >> 1, receiver & 1] = second
     kept_one[...] = slots_one[0, 0]
-    swapped_one[...] = slots_one[0, 1]
-    across_one[...] = slots_one[1, 0]
+    swapped_one[...] = slots_one[1, 0]
+    across_one[...] = slots_one[0, 1]
     diagonal_one[...] = slots_one[1, 1]
     kept_two[...] = slots_two[0]
     swapped_two[...] = slots_two[1]
@@ -103,36 +105,38 @@
     factors[:, rank:] = product(left_two[...], middle_two[0, 0])
 
 
-def put(stacked, apart, rows):
-    row = pl.multiple_of((lax.axis_index("grp") ^ apart) * rows.shape[0], rows.shape[0])
-    stacked[pl.ds(row, rows.shape[0])] = rows
-
-
-def regroup_one(*refs):
-    stacked = refs[-1]
-    half = (len(refs) - 1) // 2
+def combine(factors, *refs):
+    levels, (out, stacked) = refs[:-2], refs[-2:]
+    me = lax.axis_index("grp")
     quarter = lax.axis_index("quarter")
-    for n in range(half):
-        for other in range(2):
-            put(stacked, 4 * n + 2 * quarter + other, refs[n][other])
-            put(stacked, 4 * n + 2 * (1 - quarter) + other, refs[half + n][other])
-
-
-def combine(factors, first, other_second, *refs):
-    second, (out, stacked) = refs[:-2], refs[-2:]
-    core = lax.axis_index("grp") & 1
-    for n in range(len(second)):
-        for other in range(2):
-            put(stacked, 4 * n + 2 * core + other, second[n][other, core])
-            put(stacked, 4 * n + 2 * (1 - core) + 1 - other, other_second[n, other])
-    rank = first.shape[0]
-    out[...] = product(factors[:, :rank], first[...]) + product(factors[:, rank:], stacked[...])
+    core = me & 1
+    rank = factors.shape[1] // 2
+    quads = (len(levels) - 2) // 4
+    straight, diagonal, second = levels[:quads], levels[quads : 2 * quads], levels[2 * quads : -2]
+    other_first, other_second = levels[-2:]
+    part = other_first.shape[2]
+
+    def put(level, apart, sender, rows):
+        row = pl.multiple_of(level * rank + (me ^ (2 * apart + sender)) * part, part)
+        stacked[pl.ds(row, part)] = rows
+
+    for sender in range(2):
+        for n in range(quads):
+            mine, others = 4 * n + 2 * core, 4 * n + 2 * (1 - core)
+            put(0, mine + quarter, sender, straight[n][sender, core])
+            put(0, mine + 1 - quarter, sender, diagonal[n][sender, core])
+            put(0, others + quarter, 1 - sender, other_first[n, sender])
+            put(0, others + 1 - quarter, 1 - sender, other_first[quads + n, sender])
+        for n in range(2 * quads):
+            put(1, 2 * n + core, sender, second[n][sender, core])
+            put(1, 2 * n + 1 - core, 1 - sender, other_second[n, sender])
+    out[...] = product(factors[...], stacked[...])
 
 
 def near(mesh, rhs, left_one, left_two, middle_one, middle_two, right_one, right_two, order_one, order_two):
     groups = mesh.shape["grp"]
     chips = groups // 2
-    half = chips // 2
+    quads = chips // 4
     rank, columns = right_one.shape[1], rhs.shape[1]
     part = rank // groups
 
@@ -169,15 +173,16 @@
     def swap_quarters(value):
         return send(value, lambda h, q, g: (h, 1 - q, g))
 
+    message = f32(2, 2, part, columns)
     kept_one, swapped_one, across_one, diagonal_one, kept_two, swapped_two = call(
         project,
-        [f32(half, part, columns)] * 4 + [f32(half, 2, part, columns)] * 2,
+        [f32(quads, 2, part, columns)] * 4 + [f32(2 * quads, 2, part, columns)] * 2,
         *(in_hbm(value) for value in (order_one, order_two, rhs, right_one, right_two)),
         scratch=[
             pltpu.VMEM(rhs.shape, jnp.float32),
             pltpu.VMEM((right_one.shape[0], 2 * rank), jnp.float32),
-            pltpu.VMEM((2, 2, half, part, columns), jnp.float32),
-            pltpu.VMEM((2, half, 2, part, columns), jnp.float32),
+            pltpu.VMEM((2, 2, quads, 2, part, columns), jnp.float32),
+            pltpu.VMEM((2, 2 * quads, 2, part, columns), jnp.float32),
             pltpu.SMEM((2, *order_one.shape), jnp.int32),
             pltpu.SemaphoreType.DMA((5,)),
         ],
@@ -186,29 +191,40 @@
     diagonal_one = send(diagonal_one, lambda h, q, g: (h, 1 - q, g ^ 1))
     swapped_two = swap_cores(swapped_two)
     swapped_one = swap_cores(swapped_one)
-    messages_two = call(pair_up, [f32(2, 2, part, columns)] * half, kept_two, swapped_two, after=(swapped_one,))
+    messages_two = call(
+        pair_up, [message] * (2 * quads), kept_two, swapped_two, after=(swapped_one,)
+    )
     second = [
-        send(messages_two[n], lambda h, q, g, n=n: (h, 1 - q, g ^ (2 * (2 * n + (g & 1)))))
-        for n in range(half)
+        send(messages_two[n], lambda h, q, g, n=n: (h, 1 - q, g ^ (2 * (2 * n + g % 2))))
+        for n in range(2 * quads)
     ]
     messages_one = call(
-        add_up, [f32(2, part, columns)] * half, kept_one, swapped_one, across_one, diagonal_one, after=(messages_two[0],), cost=COST
-    )
-    first = [
-        send(messages_one[n], lambda h, q, g, n=n: (1 - h, q, g ^ (2 * (2 * n + q))))
-        for n in range(half)
-    ]
-    other_first = [swap_quarters(value) for value in first]
-    other_second = swap_cores(call(pack_other, f32(half, 2, part, columns), *second))
+        add_up,
+        [message] * quads,
+        *(kept_one, swapped_one, across_one, diagonal_one),
+        after=(messages_two[0],),
+        cost=COST,
+    )
+    straight, diagonal = (
+        [
+            send(
+                messages_one[n],
+                lambda h, q, g, n=n: (1 - h, q ^ other, g ^ (2 * (4 * n + 2 * (g % 2) + q))),
+            )
+            for n in range(quads)
+        ]
+        for other in range(2)
+    )
+    other_second = swap_cores(call(pack_other, f32(2 * quads, 2, part, columns), *second))
+    other_first = swap_cores(call(pack_other, f32(2 * quads, 2, part, columns), *straight, *diagonal, after=(other_second,)))
     factors = call(
         outer_factors, f32(left_one.shape[0], 2 * rank), left_one, middle_one, left_two, middle_two
     )
-    stacked = call(regroup_one, f32(rank, columns), *first, *other_first, cost=COST)
     return call(
         combine,
         f32(left_one.shape[0], columns),
-        *(factors, stacked, other_second, *second),
-        scratch=[pltpu.VMEM((rank, columns), jnp.float32)],
+        *(factors, *straight, *diagonal, *second, other_first, other_second),
+        scratch=[pltpu.VMEM((2 * rank, columns), jnp.float32)],
     )
 
 
@@ -256,7 +272,7 @@
         P(("half", "quarter"), "grp", None),
     )
     groups = mesh.shape["grp"]
-    direct = groups >= 4 and groups & (groups - 1) == 0 and groups // 2 <= MOST_CHIPS
+    direct = groups >= 8 and groups & (groups - 1) == 0 and groups // 2 <= MOST_CHIPS
     return jax.shard_map(
         functools.partial(near if direct else far, mesh),
         mesh=mesh,

time: 25.7 us -> 24.9 us (0.969)
  starting transfers between devices: 17 us -> 12.2 us
  waiting for transfers between devices: 5.02 us -> 9.31 us
    ppermute x11 -> x10, starting transfers between devices: 17 us -> 12.2 us  [send(): return lax.ppermute(value, AXES, pairs)]
    ppermute x11 -> x10, waiting for transfers between devices: 5.02 us -> 9.31 us  [send(): return lax.ppermute(value, AXES, pairs)]
  transfers between devices with their start and end apart: 11 -> 10, of which waited for: 3 -> 6; matrix products, arithmetic and copies ran while one was open for 0% -> 0% of each run, Pallas kernels for 1% -> 1%
where the time goes in v4:
time: 24.9 us; the launch traced here: 24.8 us
  starting transfers between devices  12.2 us (49%)
  waiting for transfers between devices  9.31 us (37%)
  Pallas kernels  3.19 us (13%)
    ppermute x10, starting transfers between devices, send(): return lax.ppermute(value, AXES, pairs)  12.2 us
    ppermute x10, waiting for transfers between devices, send(): return lax.ppermute(value, AXES, pairs)  9.31 us
    pallas_call x7, Pallas kernels, call(): pl.pallas_call(body, out_shape=out_shape, in_specs=[HBM if kernel is proj...  3.19 us
  transfers between devices with their start and end apart: 10, of which 6 were waited for; matrix products, arithmetic and copies ran while one was open for 0% of the time, Pallas kernels for 1%

profile of v4, /device:TPU:0, one launch (start us, length us, event | category | flops | bytes accessed | tf_op | source)
XLA Modules:
  0.0 24.8 jit_solution(18162419241773950942)
XLA Ops:
  0.0 1.7 %shard_map.92 = (f32[1,2,16,512]{3,2,1,0:T(8,128)S(1)}, f32[1,2,16,512]{3,2,1,0:T(8,128)S(1)}, f32[1,2,16,512]{3,2,1,0:T(8,128)S(1)}, f32[1,2,16,512]{3,2,1,0:T(...) custom-call(s32[1,1,8]{2,1,0:T(1,128)} %refs_0_.3, s32[1,1,8]{2,1,0:T(1,128)} %refs_1_.3, ...), custom_call_target="tpu_custom_call" | custom-call | tf_op jit(solution)/shard_map/pallas_call | solution.py:149
  1.7 0.5 %collective-permute-start.3 = (f32[2,2,16,512]{3,2,1,0:T(8,128)S(1)}, f32[2,2,16,512]{3,2,1,0:T(8,128)S(1)}, u32[]{:S(2)}, u32[]{:S(2)}) collective-permute-start(f32[2,2,16,512]{3,2,1,0:T(8,128)S(1)} %get-tuple-element.18), channel_id=1, source_target_pairs={{0,1},{1,0},{2,3},{3,2},{4,5},{5,4},{6,7},{7,6},{8,9},{9,8},{10,11... | collective-permute-start | bytes 393224 | tf_op jit(solution)/shard_map/ppermute | solution.py:168
  2.2 0.1 collective-permute-start
  2.3 2.9 %collective-permute-start.1 = (f32[1,2,16,512]{3,2,1,0:T(8,128)S(1)}, f32[1,2,16,512]{3,2,1,0:T(8,128)S(1)}, u32[]{:S(2)}, u32[]{:S(2)}) collective-permute-start(f32[1,2,16,512]{3,2,1,0:T(8,128)S(1)} %get-tuple-element.15), channel_id=1, source_target_pairs={{0,8},{1,9},{2,10},{3,11},{4,12},{5,13},{6,14},{7,15},{8,0},{9,1},... | collective-permute-start | bytes 196616 | tf_op jit(solution)/shard_map/ppermute | solution.py:168
  5.2 0.0 collective-permute-start.2
  5.2 0.0 collective-permute-done.refs_2_.refs_1_
  5.2 0.0 collective-permute-done.3.refs_1_
  5.3 3.5 %collective-permute-start.7 = (f32[2,2,16,512]{3,2,1,0:T(8,128)S(1)}, f32[2,2,16,512]{3,2,1,0:T(8,128)S(1)}, u32[]{:S(2)}, u32[]{:S(2)}) collective-permute-start(f32[2,2,16,512]{3,2,1,0:T(8,128)S(1)} %get-tuple-element.20), channel_id=1, source_target_pairs={{0,12},{1,15},{2,14},{3,13},{4,8},{5,11},{6,10},{7,9},{8,4},{9,7},... | collective-permute-start | bytes 393224 | tf_op jit(solution)/shard_map/ppermute | solution.py:168
  8.8 0.6 %collective-permute-start.6 = (f32[2,2,16,512]{3,2,1,0:T(8,128)S(1)}, f32[2,2,16,512]{3,2,1,0:T(8,128)S(1)}, u32[]{:S(2)}, u32[]{:S(2)}) collective-permute-start(f32[2,2,16,512]{3,2,1,0:T(8,128)S(1)} %get-tuple-element.19.refs_4_), channel_id=1, source_target_pairs={{0,8},{1,11},{2,10},{3,9},{4,12},{5,15},{6,14},{7,13},{8,0},{9,3},... | collective-permute-start | bytes 393224 | tf_op jit(solution)/shard_map/ppermute | solution.py:168
  9.4 0.0 collective-permute-done.1.refs_2_
  9.4 0.2 collective-permute-done.2.refs_3_
  9.6 2.2 %collective-permute-start.5 = (f32[2,2,16,512]{3,2,1,0:T(8,128)S(1)}, f32[2,2,16,512]{3,2,1,0:T(8,128)S(1)}, u32[]{:S(2)}, u32[]{:S(2)}) collective-permute-start(f32[2,2,16,512]{3,2,1,0:T(8,128)S(1)} %shard_map.94), channel_id=1, source_target_pairs={{0,24},{1,29},{2,26},{3,31},{4,28},{5,25},{6,30},{7,27},{8,18},{9,... | collective-permute-start | bytes 393224 | tf_op jit(solution)/shard_map/ppermute | solution.py:168
  11.8 0.5 %collective-permute-start.4 = (f32[2,2,16,512]{3,2,1,0:T(8,128)S(1)}, f32[2,2,16,512]{3,2,1,0:T(8,128)S(1)}, u32[]{:S(2)}, u32[]{:S(2)}) collective-permute-start(f32[2,2,16,512]{3,2,1,0:T(8,128)S(1)} %shard_map.94), channel_id=1, source_target_pairs={{0,16},{1,21},{2,18},{3,23},{4,20},{5,17},{6,22},{7,19},{8,26},{9,... | collective-permute-start | bytes 393224 | tf_op jit(solution)/shard_map/ppermute | solution.py:168
  12.3 4.0 %collective-permute-done.7.refs_1_.refs_4_ = f32[2,2,16,512]{3,2,1,0:T(8,128)S(1)} collective-permute-done((f32[2,2,16,512]{3,2,1,0:T(8,128)S(1)}, f32[2,2,16,512]{3,2,1,0:T(8,128)S(1)}, u32[]{:S(2)}, u32[]{:S(2)}) %collective-permute-start.7) | collective-permute-done | bytes 131104 | tf_op jit(solution)/shard_map/ppermute | solution.py:168
  16.4 3.0 %collective-permute-done.6.refs_0_.refs_3_ = f32[2,2,16,512]{3,2,1,0:T(8,128)S(1)} collective-permute-done((f32[2,2,16,512]{3,2,1,0:T(8,128)S(1)}, f32[2,2,16,512]{3,2,1,0:T(8,128)S(1)}, u32[]{:S(2)}, u32[]{:S(2)}) %collective-permute-start.6) | collective-permute-done | bytes 131104 | tf_op jit(solution)/shard_map/ppermute | solution.py:168
  19.4 0.0 copy-start
  19.4 0.0 copy-start.1
  19.4 0.0 copy-start.2
  19.4 0.0 copy-start.3
  19.4 0.1 collective-permute-start.8
  19.5 0.4 %collective-permute-done.5.refs_1_.refs_2_ = f32[2,2,16,512]{3,2,1,0:T(8,128)S(1)} collective-permute-done((f32[2,2,16,512]{3,2,1,0:T(8,128)S(1)}, f32[2,2,16,512]{3,2,1,0:T(8,128)S(1)}, u32[]{:S(2)}, u32[]{:S(2)}) %collective-permute-start.5) | collective-permute-done | bytes 131104 | tf_op jit(solution)/shard_map/ppermute | solution.py:168
  20.0 0.0 collective-permute-done.4.refs_0_.refs_1_
  20.0 0.9 %collective-permute-done.8.refs_2_.refs_6_ = f32[2,2,16,512]{3,2,1,0:T(8,128)S(1)} collective-permute-done((f32[2,2,16,512]{3,2,1,0:T(8,128)S(1)}, f32[2,2,16,512]{3,2,1,0:T(8,128)S(1)}, u32[]{:S(2)}, u32[]{:S(2)}) %collective-permute-start.8) | collective-permute-done | bytes 131104 | tf_op jit(solution)/shard_map/ppermute | solution.py:168
  20.9 1.7 %collective-permute-start.9 = (f32[2,2,16,512]{3,2,1,0:T(8,128)S(1)}, f32[2,2,16,512]{3,2,1,0:T(8,128)S(1)}, u32[]{:S(2)}, u32[]{:S(2)}) collective-permute-start(f32[2,2,16,512]{3,2,1,0:T(8,128)S(1)} %shard_map.96), channel_id=1, source_target_pairs={{0,1},{1,0},{2,3},{3,2},{4,5},{5,4},{6,7},{7,6},{8,9},{9,8},{10,11... | collective-permute-start | bytes 393224 | tf_op jit(solution)/shard_map/ppermute | solution.py:168
  22.6 0.0 copy-done
  22.6 0.0 copy-done.1
  22.6 0.0 copy-done.2
  22.6 0.0 copy-done.3
  22.6 0.2 shard_map.91.refs_0_
  22.8 0.7 %collective-permute-done.9.refs_5_ = f32[2,2,16,512]{3,2,1,0:T(8,128)S(1)} collective-permute-done((f32[2,2,16,512]{3,2,1,0:T(8,128)S(1)}, f32[2,2,16,512]{3,2,1,0:T(8,128)S(1)}, u32[]{:S(2)}, u32[]{:S(2)}) %collective-permute-start.9) | collective-permute-done | bytes 131104 | tf_op jit(solution)/shard_map/ppermute | solution.py:168
  23.5 1.2 %shard_map.97 = f32[256,512]{1,0:T(8,128)} custom-call(f32[256,256]{1,0:T(8,128)S(1)} %shard_map.91.refs_0_, f32[2,2,16,512]{3,2,1,0:T(8,128)S(1)} %collective-permute-done.4.refs_0_.refs_1_, f32[2,2,16,512]{3,2,1,0:T(8,128)S(1)} %collective-permute-done.5.refs_1_.refs_2_, f32[2,2,16,512]{3,2,1,0:T(8,128)S(1)} %collective-permute-done.6.refs_0_.refs_3_, ...), custom_call_target="tpu_custom_call" | custom-call | tf_op jit(solution)/shard_map/pallas_call | solution.py:149
  (4 shorter events, 0.1 us)
Async XLA Ops:
  1.7 3.6 %collective-permute-start.3 = (f32[2,2,16,512]{3,2,1,0:T(8,128)S(1)}, f32[2,2,16,512]{3,2,1,0:T(8,128)S(1)}, u32[]{:S(2)}, u32[]{:S(2)}) collective-permute-start(f32[2,2,16,512]{3,2,1,0:T(8,128)S(1)} %get-tuple-element.18), channel_id=1, source_target_pairs={{0,1},{1,0},{2,3},{3,2},{4,5},{5,4},{6,7},{7,6},{8,9},{9,8},{10,11... | collective-permute-start | bytes 393224 | tf_op jit(solution)/shard_map/ppermute | solution.py:168
  2.2 3.0 %collective-permute-start = (f32[1,2,16,512]{3,2,1,0:T(8,128)S(1)}, f32[1,2,16,512]{3,2,1,0:T(8,128)S(1)}, u32[]{:S(2)}, u32[]{:S(2)}) collective-permute-start(f32[1,2,16,512]{3,2,1,0:T(8,128)S(1)} %get-tuple-element.14), channel_id=1, source_target_pairs={{0,1},{1,0},{2,3},{3,2},{4,5},{5,4},{6,7},{7,6},{8,9},{9,8},{10,11... | collective-permute-start | bytes 196616 | tf_op jit(solution)/shard_map/ppermute | solution.py:168
  2.3 7.1 %collective-permute-start.1 = (f32[1,2,16,512]{3,2,1,0:T(8,128)S(1)}, f32[1,2,16,512]{3,2,1,0:T(8,128)S(1)}, u32[]{:S(2)}, u32[]{:S(2)}) collective-permute-start(f32[1,2,16,512]{3,2,1,0:T(8,128)S(1)} %get-tuple-element.15), channel_id=1, source_target_pairs={{0,8},{1,9},{2,10},{3,11},{4,12},{5,13},{6,14},{7,15},{8,0},{9,1},... | collective-permute-start | bytes 196616 | tf_op jit(solution)/shard_map/ppermute | solution.py:168
  5.2 4.4 %collective-permute-start.2 = (f32[1,2,16,512]{3,2,1,0:T(8,128)S(1)}, f32[1,2,16,512]{3,2,1,0:T(8,128)S(1)}, u32[]{:S(2)}, u32[]{:S(2)}) collective-permute-start(f32[1,2,16,512]{3,2,1,0:T(8,128)S(1)} %get-tuple-element.16), channel_id=1, source_target_pairs={{0,9},{1,8},{2,11},{3,10},{4,13},{5,12},{6,15},{7,14},{8,1},{9,0},... | collective-permute-start | bytes 196616 | tf_op jit(solution)/shard_map/ppermute | solution.py:168
  5.3 11.1 %collective-permute-start.7 = (f32[2,2,16,512]{3,2,1,0:T(8,128)S(1)}, f32[2,2,16,512]{3,2,1,0:T(8,128)S(1)}, u32[]{:S(2)}, u32[]{:S(2)}) collective-permute-start(f32[2,2,16,512]{3,2,1,0:T(8,128)S(1)} %get-tuple-element.20), channel_id=1, source_target_pairs={{0,12},{1,15},{2,14},{3,13},{4,8},{5,11},{6,10},{7,9},{8,4},{9,7},... | collective-permute-start | bytes 393224 | tf_op jit(solution)/shard_map/ppermute | solution.py:168
  8.8 10.6 %collective-permute-start.6 = (f32[2,2,16,512]{3,2,1,0:T(8,128)S(1)}, f32[2,2,16,512]{3,2,1,0:T(8,128)S(1)}, u32[]{:S(2)}, u32[]{:S(2)}) collective-permute-start(f32[2,2,16,512]{3,2,1,0:T(8,128)S(1)} %get-tuple-element.19.refs_4_), channel_id=1, source_target_pairs={{0,8},{1,11},{2,10},{3,9},{4,12},{5,15},{6,14},{7,13},{8,0},{9,3},... | collective-permute-start | bytes 393224 | tf_op jit(solution)/shard_map/ppermute | solution.py:168
  9.6 10.4 %collective-permute-start.5 = (f32[2,2,16,512]{3,2,1,0:T(8,128)S(1)}, f32[2,2,16,512]{3,2,1,0:T(8,128)S(1)}, u32[]{:S(2)}, u32[]{:S(2)}) collective-permute-start(f32[2,2,16,512]{3,2,1,0:T(8,128)S(1)} %shard_map.94), channel_id=1, source_target_pairs={{0,24},{1,29},{2,26},{3,31},{4,28},{5,25},{6,30},{7,27},{8,18},{9,... | collective-permute-start | bytes 393224 | tf_op jit(solution)/shard_map/ppermute | solution.py:168
  11.8 8.2 %collective-permute-start.4 = (f32[2,2,16,512]{3,2,1,0:T(8,128)S(1)}, f32[2,2,16,512]{3,2,1,0:T(8,128)S(1)}, u32[]{:S(2)}, u32[]{:S(2)}) collective-permute-start(f32[2,2,16,512]{3,2,1,0:T(8,128)S(1)} %shard_map.94), channel_id=1, source_target_pairs={{0,16},{1,21},{2,18},{3,23},{4,20},{5,17},{6,22},{7,19},{8,26},{9,... | collective-permute-start | bytes 393224 | tf_op jit(solution)/shard_map/ppermute | solution.py:168
  19.4 3.2 %copy-start = (f32[256,128]{1,0:T(8,128)S(1)}, f32[256,128]{1,0:T(8,128)}, u32[]{:S(2)}) copy-start(f32[256,128]{1,0:T(8,128)} %refs_0_.2) | copy-start | bytes 393220
  19.4 3.2 %copy-start.1 = (f32[256,128]{1,0:T(8,128)S(1)}, f32[256,128]{1,0:T(8,128)}, u32[]{:S(2)}) copy-start(f32[256,128]{1,0:T(8,128)} %refs_2_.2) | copy-start | bytes 393220
  19.4 3.1 %copy-start.2 = (f32[1,1,128,128]{3,2,1,0:T(8,128)S(1)}, f32[1,1,128,128]{3,2,1,0:T(8,128)}, u32[]{:S(2)}) copy-start(f32[1,1,128,128]{3,2,1,0:T(8,128)} %refs_1_.2) | copy-start | bytes 196612
  19.4 3.1 %copy-start.3 = (f32[1,1,128,128]{3,2,1,0:T(8,128)S(1)}, f32[1,1,128,128]{3,2,1,0:T(8,128)}, u32[]{:S(2)}) copy-start(f32[1,1,128,128]{3,2,1,0:T(8,128)} %refs_3_.2) | copy-start | bytes 196612
  19.4 1.4 %collective-permute-start.8 = (f32[2,2,16,512]{3,2,1,0:T(8,128)S(1)}, f32[2,2,16,512]{3,2,1,0:T(8,128)S(1)}, u32[]{:S(2)}, u32[]{:S(2)}) collective-permute-start(f32[2,2,16,512]{3,2,1,0:T(8,128)S(1)} %shard_map.95), channel_id=1, source_target_pairs={{0,1},{1,0},{2,3},{3,2},{4,5},{5,4},{6,7},{7,6},{8,9},{9,8},{10,11... | collective-permute-start | bytes 393224 | tf_op jit(solution)/shard_map/ppermute | solution.py:168
  20.9 2.7 %collective-permute-start.9 = (f32[2,2,16,512]{3,2,1,0:T(8,128)S(1)}, f32[2,2,16,512]{3,2,1,0:T(8,128)S(1)}, u32[]{:S(2)}, u32[]{:S(2)}) collective-permute-start(f32[2,2,16,512]{3,2,1,0:T(8,128)S(1)} %shard_map.96), channel_id=1, source_target_pairs={{0,1},{1,0},{2,3},{3,2},{4,5},{5,4},{6,7},{7,6},{8,9},{9,8},{10,11... | collective-permute-start | bytes 393224 | tf_op jit(solution)/shard_map/ppermute | solution.py:168

commit v5 on v4

--- a/solution.py
+++ b/solution.py
@@ -10,6 +10,8 @@
 AXES = ("half", "quarter", "grp")
 MOST_CHIPS = 8
 COST = 10**10
+TABLE = ((3, 1), (0, 2))
+COLUMN_BLOCKS = 1
 PARAMS = pltpu.CompilerParams(vmem_limit_bytes=16 * 2**20)
 VMEM = pl.BlockSpec(memory_space=pltpu.VMEM)
 ANY = pl.BlockSpec(memory_space=pl.ANY)
@@ -31,13 +33,9 @@
     return high, low
 
 
-def product(left, right, dims=((1,), (0,))):
-    dot = functools.partial(
-        lax.dot_general,
-        dimension_numbers=(dims, ((), ())),
-        preferred_element_type=jnp.float32,
-    )
-    (lh, ll), (rh, rl) = split(left), split(right)
+def product(left, right):
+    dot = functools.partial(jnp.dot, preferred_element_type=jnp.float32)
+    (lh, ll), (rh, rl) = left, split(right)
     return dot(lh, rh) + (dot(lh, rl) + dot(ll, rh))
 
 
@@ -50,28 +48,40 @@
     pairs = (
         (right_one, rights.at[:, :rank]),
         (right_two, rights.at[:, rank:]),
-        (rhs, values),
         (order_one, orders.at[0]),
         (order_two, orders.at[1]),
     )
+    width = rhs.shape[1] // COLUMN_BLOCKS
+    blocks = [pl.ds(n * width, width) for n in range(COLUMN_BLOCKS)]
+    pairs += tuple((rhs.at[:, block], values.at[:, block]) for block in blocks)
     copies = [pltpu.make_async_copy(*pair, sems.at[n]) for n, pair in enumerate(pairs)]
     for copy in copies:
         copy.start()
     me = lax.axis_index("grp")
     quarter = lax.axis_index("quarter")
-    for copy in copies:
+    for copy in copies[:4]:
         copy.wait()
-    coeffs = product(rights[...], values[...], ((0,), (0,)))
+    left = split(rights[...].T)
     part = slots_one.shape[4]
-    for p in range(rank // part):
-        first, second = (coeffs[n * rank + p * part : n * rank + (p + 1) * part] for n in range(2))
-        receiver = orders[0, 0, 0, p]
-        apart = (receiver >> 1) ^ (me >> 1)
-        core = ((apart >> 1) ^ me) & 1
-        slots_one[core, (apart ^ quarter) & 1, apart >> 2, receiver & 1] = first
-        receiver = orders[1, 0, 0, p]
-        apart = (receiver >> 1) ^ (me >> 1)
-        slots_two[(apart ^ me) & 1, apart >> 1, receiver & 1] = second
+    for copy, block in zip(copies[4:], blocks):
+        copy.wait()
+        coeffs = product(left, values[:, block])
+        for p in range(rank // part):
+            first, second = (
+                coeffs[n * rank + p * part : n * rank + (p + 1) * part] for n in range(2)
+            )
+            receiver = orders[0, 0, 0, p]
+            apart = (receiver >> 1) ^ (me >> 1)
+            core = ((apart >> 1) ^ me) & 1
+            slots_one[core, (apart ^ quarter) & 1, apart >> 2, receiver & 1, :, block] = first
+            receiver = orders[1, 0, 0, p]
+            apart = (receiver >> 1) ^ (me >> 1)
+            core, place = 0, 0
+            for c in range(2):
+                for m in range(2):
+                    core = jnp.where((apart & 3) == TABLE[c][m], c, core)
+                    place = jnp.where((apart & 3) == TABLE[c][m], m, place)
+            slots_two[(core ^ me) & 1, (apart >> 2) * 2 + place, receiver & 1, :, block] = second
     kept_one[...] = slots_one[0, 0]
     swapped_one[...] = slots_one[1, 0]
     across_one[...] = slots_one[0, 1]
@@ -101,8 +111,8 @@
 
 def outer_factors(left_one, middle_one, left_two, middle_two, factors):
     rank = left_one.shape[1]
-    factors[:, :rank] = product(left_one[...], middle_one[0, 0])
-    factors[:, rank:] = product(left_two[...], middle_two[0, 0])
+    factors[:, :rank] = product(split(left_one[...]), middle_one[0, 0])
+    factors[:, rank:] = product(split(left_two[...]), middle_two[0, 0])
 
 
 def combine(factors, *refs):
@@ -128,9 +138,12 @@
             put(0, others + quarter, 1 - sender, other_first[n, sender])
             put(0, others + 1 - quarter, 1 - sender, other_first[quads + n, sender])
         for n in range(2 * quads):
-            put(1, 2 * n + core, sender, second[n][sender, core])
-            put(1, 2 * n + 1 - core, 1 - sender, other_second[n, sender])
-    out[...] = product(factors[...], stacked[...])
+            here, there = (
+                4 * (n // 2) + jnp.where(core == c, TABLE[1][n % 2], TABLE[0][n % 2]) for c in (1, 0)
+            )
+            put(1, here, sender, second[n][sender, core])
+            put(1, there, 1 - sender, other_second[n, sender])
+    out[...] = product(split(factors[...]), stacked[...])
 
 
 def near(mesh, rhs, left_one, left_two, middle_one, middle_two, right_one, right_two, order_one, order_two):
@@ -184,7 +197,7 @@
             pltpu.VMEM((2, 2, quads, 2, part, columns), jnp.float32),
             pltpu.VMEM((2, 2 * quads, 2, part, columns), jnp.float32),
             pltpu.SMEM((2, *order_one.shape), jnp.int32),
-            pltpu.SemaphoreType.DMA((5,)),
+            pltpu.SemaphoreType.DMA((4 + COLUMN_BLOCKS,)),
         ],
     )
     across_one = swap_quarters(across_one)
@@ -195,7 +208,7 @@
         pair_up, [message] * (2 * quads), kept_two, swapped_two, after=(swapped_one,)
     )
     second = [
-        send(messages_two[n], lambda h, q, g, n=n: (h, 1 - q, g ^ (2 * (2 * n + g % 2))))
+        send(messages_two[n], lambda h, q, g, n=n: (h, 1 - q, g ^ (2 * (4 * (n // 2) + TABLE[g % 2][n % 2]))))
         for n in range(2 * quads)
     ]
     messages_one = call(
@@ -232,7 +245,7 @@
     part = slots_one.shape[1]
     levels = ((order_one, right_one, slots_one), (order_two, right_two, slots_two))
     for order, right, slots in levels:
-        coeffs = product(right[...], rhs[...], ((0,), (0,)))
+        coeffs = product(split(right[...].T), rhs[...])
         for p in range(order.shape[2]):
             slots[order[0, 0, p]] = coeffs[p * part : (p + 1) * part]
 

time: 24.9 us -> 23.8 us (0.956)
  waiting for transfers between devices: 9.31 us -> 5.71 us
  starting transfers between devices: 12.2 us -> 14.6 us
    ppermute x10, waiting for transfers between devices: 9.31 us -> 5.71 us  [send(): return lax.ppermute(value, AXES, pairs)]
    ppermute x10, starting transfers between devices: 12.2 us -> 14.6 us  [send(): return lax.ppermute(value, AXES, pairs)]
  transfers between devices with their start and end apart: 10 -> 10, of which waited for: 6 -> 4; matrix products, arithmetic and copies ran while one was open for 0% -> 0% of each run, Pallas kernels for 1% -> 1%
where the time goes in v5:
time: 23.8 us; the launch traced here: 23.5 us
  starting transfers between devices  14.6 us (61%)
  waiting for transfers between devices  5.71 us (24%)
  Pallas kernels  3.15 us (13%)
    ppermute x10, starting transfers between devices, send(): return lax.ppermute(value, AXES, pairs)  14.6 us
    ppermute x10, waiting for transfers between devices, send(): return lax.ppermute(value, AXES, pairs)  5.71 us
    pallas_call x7, Pallas kernels, call(): pl.pallas_call(body, out_shape=out_shape, in_specs=[HBM if kernel is proj...  3.15 us
  transfers between devices with their start and end apart: 10, of which 4 were waited for; matrix products, arithmetic and copies ran while one was open for 0% of the time, Pallas kernels for 1%

profile of v5, /device:TPU:0, one launch (start us, length us, event | category | flops | bytes accessed | tf_op | source)
XLA Modules:
  0.0 23.5 jit_solution(16865115229046955948)
XLA Ops:
  0.0 1.6 %shard_map.92 = (f32[1,2,16,512]{3,2,1,0:T(8,128)S(1)}, f32[1,2,16,512]{3,2,1,0:T(8,128)S(1)}, f32[1,2,16,512]{3,2,1,0:T(8,128)S(1)}, f32[1,2,16,512]{3,2,1,0:T(...) custom-call(s32[1,1,8]{2,1,0:T(1,128)} %refs_0_.3, s32[1,1,8]{2,1,0:T(1,128)} %refs_1_.3, ...), custom_call_target="tpu_custom_call" | custom-call | tf_op jit(solution)/shard_map/pallas_call | solution.py:162
  1.6 0.5 %collective-permute-start.3 = (f32[2,2,16,512]{3,2,1,0:T(8,128)S(1)}, f32[2,2,16,512]{3,2,1,0:T(8,128)S(1)}, u32[]{:S(2)}, u32[]{:S(2)}) collective-permute-start(f32[2,2,16,512]{3,2,1,0:T(8,128)S(1)} %get-tuple-element.18), channel_id=1, source_target_pairs={{0,1},{1,0},{2,3},{3,2},{4,5},{5,4},{6,7},{7,6},{8,9},{9,8},{10,11... | collective-permute-start | bytes 393224 | tf_op jit(solution)/shard_map/ppermute | solution.py:181
  2.2 0.1 collective-permute-start
  2.2 2.9 %collective-permute-start.1 = (f32[1,2,16,512]{3,2,1,0:T(8,128)S(1)}, f32[1,2,16,512]{3,2,1,0:T(8,128)S(1)}, u32[]{:S(2)}, u32[]{:S(2)}) collective-permute-start(f32[1,2,16,512]{3,2,1,0:T(8,128)S(1)} %get-tuple-element.15), channel_id=1, source_target_pairs={{0,8},{1,9},{2,10},{3,11},{4,12},{5,13},{6,14},{7,15},{8,0},{9,1},... | collective-permute-start | bytes 196616 | tf_op jit(solution)/shard_map/ppermute | solution.py:181
  5.2 0.0 collective-permute-start.2
  5.2 0.0 collective-permute-done.refs_2_.refs_1_
  5.2 0.0 collective-permute-done.3.refs_1_
  5.2 2.5 %collective-permute-start.7 = (f32[2,2,16,512]{3,2,1,0:T(8,128)S(1)}, f32[2,2,16,512]{3,2,1,0:T(8,128)S(1)}, u32[]{:S(2)}, u32[]{:S(2)}) collective-permute-start(f32[2,2,16,512]{3,2,1,0:T(8,128)S(1)} %get-tuple-element.20), channel_id=1, source_target_pairs={{0,10},{1,13},{2,8},{3,15},{4,14},{5,9},{6,12},{7,11},{8,2},{9,5},... | collective-permute-start | bytes 393224 | tf_op jit(solution)/shard_map/ppermute | solution.py:181
  7.7 2.5 %collective-permute-start.6 = (f32[2,2,16,512]{3,2,1,0:T(8,128)S(1)}, f32[2,2,16,512]{3,2,1,0:T(8,128)S(1)}, u32[]{:S(2)}, u32[]{:S(2)}) collective-permute-start(f32[2,2,16,512]{3,2,1,0:T(8,128)S(1)} %get-tuple-element.19.refs_4_), channel_id=1, source_target_pairs={{0,14},{1,9},{2,12},{3,11},{4,10},{5,13},{6,8},{7,15},{8,6},{9,1},... | collective-permute-start | bytes 393224 | tf_op jit(solution)/shard_map/ppermute | solution.py:181
  10.2 0.0 collective-permute-done.1.refs_2_
  10.2 0.0 collective-permute-done.2.refs_3_
  10.3 2.4 %collective-permute-start.5 = (f32[2,2,16,512]{3,2,1,0:T(8,128)S(1)}, f32[2,2,16,512]{3,2,1,0:T(8,128)S(1)}, u32[]{:S(2)}, u32[]{:S(2)}) collective-permute-start(f32[2,2,16,512]{3,2,1,0:T(8,128)S(1)} %shard_map.94), channel_id=1, source_target_pairs={{0,24},{1,29},{2,26},{3,31},{4,28},{5,25},{6,30},{7,27},{8,18},{9,... | collective-permute-start | bytes 393224 | tf_op jit(solution)/shard_map/ppermute | solution.py:181
  12.7 0.5 %collective-permute-start.4 = (f32[2,2,16,512]{3,2,1,0:T(8,128)S(1)}, f32[2,2,16,512]{3,2,1,0:T(8,128)S(1)}, u32[]{:S(2)}, u32[]{:S(2)}) collective-permute-start(f32[2,2,16,512]{3,2,1,0:T(8,128)S(1)} %shard_map.94), channel_id=1, source_target_pairs={{0,16},{1,21},{2,18},{3,23},{4,20},{5,17},{6,22},{7,19},{8,26},{9,... | collective-permute-start | bytes 393224 | tf_op jit(solution)/shard_map/ppermute | solution.py:181
  13.2 0.0 collective-permute-done.7.refs_1_.refs_4_
  13.2 2.3 %collective-permute-done.6.refs_0_.refs_3_ = f32[2,2,16,512]{3,2,1,0:T(8,128)S(1)} collective-permute-done((f32[2,2,16,512]{3,2,1,0:T(8,128)S(1)}, f32[2,2,16,512]{3,2,1,0:T(8,128)S(1)}, u32[]{:S(2)}, u32[]{:S(2)}) %collective-permute-start.6) | collective-permute-done | bytes 131104 | tf_op jit(solution)/shard_map/ppermute | solution.py:181
  15.5 0.0 copy-start
  15.5 0.0 copy-start.1
  15.6 0.0 copy-start.2
  15.6 0.0 copy-start.3
  15.6 0.1 collective-permute-start.8
  15.7 2.2 %collective-permute-done.5.refs_1_.refs_2_ = f32[2,2,16,512]{3,2,1,0:T(8,128)S(1)} collective-permute-done((f32[2,2,16,512]{3,2,1,0:T(8,128)S(1)}, f32[2,2,16,512]{3,2,1,0:T(8,128)S(1)}, u32[]{:S(2)}, u32[]{:S(2)}) %collective-permute-start.5) | collective-permute-done | bytes 131104 | tf_op jit(solution)/shard_map/ppermute | solution.py:181
  17.9 0.5 %collective-permute-done.4.refs_0_.refs_1_ = f32[2,2,16,512]{3,2,1,0:T(8,128)S(1)} collective-permute-done((f32[2,2,16,512]{3,2,1,0:T(8,128)S(1)}, f32[2,2,16,512]{3,2,1,0:T(8,128)S(1)}, u32[]{:S(2)}, u32[]{:S(2)}) %collective-permute-start.4) | collective-permute-done | bytes 131104 | tf_op jit(solution)/shard_map/ppermute | solution.py:181
  18.3 0.0 collective-permute-done.8.refs_2_.refs_6_
  18.3 3.0 %collective-permute-start.9 = (f32[2,2,16,512]{3,2,1,0:T(8,128)S(1)}, f32[2,2,16,512]{3,2,1,0:T(8,128)S(1)}, u32[]{:S(2)}, u32[]{:S(2)}) collective-permute-start(f32[2,2,16,512]{3,2,1,0:T(8,128)S(1)} %shard_map.96), channel_id=1, source_target_pairs={{0,1},{1,0},{2,3},{3,2},{4,5},{5,4},{6,7},{7,6},{8,9},{9,8},{10,11... | collective-permute-start | bytes 393224 | tf_op jit(solution)/shard_map/ppermute | solution.py:181
  21.3 0.0 copy-done
  21.3 0.0 copy-done.1
  21.3 0.0 copy-done.2
  21.3 0.0 copy-done.3
  21.4 0.2 %shard_map.91.refs_0_ = f32[256,256]{1,0:T(8,128)S(1)} custom-call(f32[256,128]{1,0:T(8,128)S(1)} %copy-done, f32[1,1,128,128]{3,2,1,0:T(8,128)S(1)} %copy-done.2, f32[256,128]{1,0:T(8,128)S(1)} %copy-done.1, f32[1,1,128,128]{3,2,1,0:T(8,128)S(1)} %copy-done.3), custom_call_target="tpu_custom_call" | custom-call | tf_op jit(solution)/shard_map/pallas_call | solution.py:162
  21.6 0.7 %collective-permute-done.9.refs_5_ = f32[2,2,16,512]{3,2,1,0:T(8,128)S(1)} collective-permute-done((f32[2,2,16,512]{3,2,1,0:T(8,128)S(1)}, f32[2,2,16,512]{3,2,1,0:T(8,128)S(1)}, u32[]{:S(2)}, u32[]{:S(2)}) %collective-permute-start.9) | collective-permute-done | bytes 131104 | tf_op jit(solution)/shard_map/ppermute | solution.py:181
  22.3 1.2 %shard_map.97 = f32[256,512]{1,0:T(8,128)} custom-call(f32[256,256]{1,0:T(8,128)S(1)} %shard_map.91.refs_0_, f32[2,2,16,512]{3,2,1,0:T(8,128)S(1)} %collective-permute-done.4.refs_0_.refs_1_, f32[2,2,16,512]{3,2,1,0:T(8,128)S(1)} %collective-permute-done.5.refs_1_.refs_2_, f32[2,2,16,512]{3,2,1,0:T(8,128)S(1)} %collective-permute-done.6.refs_0_.refs_3_, ...), custom_call_target="tpu_custom_call" | custom-call | tf_op jit(solution)/shard_map/pallas_call | solution.py:162
  (4 shorter events, 0.1 us)
Async XLA Ops:
  1.6 3.6 %collective-permute-start.3 = (f32[2,2,16,512]{3,2,1,0:T(8,128)S(1)}, f32[2,2,16,512]{3,2,1,0:T(8,128)S(1)}, u32[]{:S(2)}, u32[]{:S(2)}) collective-permute-start(f32[2,2,16,512]{3,2,1,0:T(8,128)S(1)} %get-tuple-element.18), channel_id=1, source_target_pairs={{0,1},{1,0},{2,3},{3,2},{4,5},{5,4},{6,7},{7,6},{8,9},{9,8},{10,11... | collective-permute-start | bytes 393224 | tf_op jit(solution)/shard_map/ppermute | solution.py:181
  2.2 3.0 %collective-permute-start = (f32[1,2,16,512]{3,2,1,0:T(8,128)S(1)}, f32[1,2,16,512]{3,2,1,0:T(8,128)S(1)}, u32[]{:S(2)}, u32[]{:S(2)}) collective-permute-start(f32[1,2,16,512]{3,2,1,0:T(8,128)S(1)} %get-tuple-element.14), channel_id=1, source_target_pairs={{0,1},{1,0},{2,3},{3,2},{4,5},{5,4},{6,7},{7,6},{8,9},{9,8},{10,11... | collective-permute-start | bytes 196616 | tf_op jit(solution)/shard_map/ppermute | solution.py:181
  2.2 8.0 %collective-permute-start.1 = (f32[1,2,16,512]{3,2,1,0:T(8,128)S(1)}, f32[1,2,16,512]{3,2,1,0:T(8,128)S(1)}, u32[]{:S(2)}, u32[]{:S(2)}) collective-permute-start(f32[1,2,16,512]{3,2,1,0:T(8,128)S(1)} %get-tuple-element.15), channel_id=1, source_target_pairs={{0,8},{1,9},{2,10},{3,11},{4,12},{5,13},{6,14},{7,15},{8,0},{9,1},... | collective-permute-start | bytes 196616 | tf_op jit(solution)/shard_map/ppermute | solution.py:181
  5.2 5.1 %collective-permute-start.2 = (f32[1,2,16,512]{3,2,1,0:T(8,128)S(1)}, f32[1,2,16,512]{3,2,1,0:T(8,128)S(1)}, u32[]{:S(2)}, u32[]{:S(2)}) collective-permute-start(f32[1,2,16,512]{3,2,1,0:T(8,128)S(1)} %get-tuple-element.16), channel_id=1, source_target_pairs={{0,9},{1,8},{2,11},{3,10},{4,13},{5,12},{6,15},{7,14},{8,1},{9,0},... | collective-permute-start | bytes 196616 | tf_op jit(solution)/shard_map/ppermute | solution.py:181
  5.2 8.0 %collective-permute-start.7 = (f32[2,2,16,512]{3,2,1,0:T(8,128)S(1)}, f32[2,2,16,512]{3,2,1,0:T(8,128)S(1)}, u32[]{:S(2)}, u32[]{:S(2)}) collective-permute-start(f32[2,2,16,512]{3,2,1,0:T(8,128)S(1)} %get-tuple-element.20), channel_id=1, source_target_pairs={{0,10},{1,13},{2,8},{3,15},{4,14},{5,9},{6,12},{7,11},{8,2},{9,5},... | collective-permute-start | bytes 393224 | tf_op jit(solution)/shard_map/ppermute | solution.py:181
  7.7 7.8 %collective-permute-start.6 = (f32[2,2,16,512]{3,2,1,0:T(8,128)S(1)}, f32[2,2,16,512]{3,2,1,0:T(8,128)S(1)}, u32[]{:S(2)}, u32[]{:S(2)}) collective-permute-start(f32[2,2,16,512]{3,2,1,0:T(8,128)S(1)} %get-tuple-element.19.refs_4_), channel_id=1, source_target_pairs={{0,14},{1,9},{2,12},{3,11},{4,10},{5,13},{6,8},{7,15},{8,6},{9,1},... | collective-permute-start | bytes 393224 | tf_op jit(solution)/shard_map/ppermute | solution.py:181
  10.3 7.6 %collective-permute-start.5 = (f32[2,2,16,512]{3,2,1,0:T(8,128)S(1)}, f32[2,2,16,512]{3,2,1,0:T(8,128)S(1)}, u32[]{:S(2)}, u32[]{:S(2)}) collective-permute-start(f32[2,2,16,512]{3,2,1,0:T(8,128)S(1)} %shard_map.94), channel_id=1, source_target_pairs={{0,24},{1,29},{2,26},{3,31},{4,28},{5,25},{6,30},{7,27},{8,18},{9,... | collective-permute-start | bytes 393224 | tf_op jit(solution)/shard_map/ppermute | solution.py:181
  12.7 5.6 %collective-permute-start.4 = (f32[2,2,16,512]{3,2,1,0:T(8,128)S(1)}, f32[2,2,16,512]{3,2,1,0:T(8,128)S(1)}, u32[]{:S(2)}, u32[]{:S(2)}) collective-permute-start(f32[2,2,16,512]{3,2,1,0:T(8,128)S(1)} %shard_map.94), channel_id=1, source_target_pairs={{0,16},{1,21},{2,18},{3,23},{4,20},{5,17},{6,22},{7,19},{8,26},{9,... | collective-permute-start | bytes 393224 | tf_op jit(solution)/shard_map/ppermute | solution.py:181
  15.5 5.8 %copy-start = (f32[256,128]{1,0:T(8,128)S(1)}, f32[256,128]{1,0:T(8,128)}, u32[]{:S(2)}) copy-start(f32[256,128]{1,0:T(8,128)} %refs_0_.2) | copy-start | bytes 393220
  15.5 5.8 %copy-start.1 = (f32[256,128]{1,0:T(8,128)S(1)}, f32[256,128]{1,0:T(8,128)}, u32[]{:S(2)}) copy-start(f32[256,128]{1,0:T(8,128)} %refs_2_.2) | copy-start | bytes 393220
  15.6 5.8 %copy-start.2 = (f32[1,1,128,128]{3,2,1,0:T(8,128)S(1)}, f32[1,1,128,128]{3,2,1,0:T(8,128)}, u32[]{:S(2)}) copy-start(f32[1,1,128,128]{3,2,1,0:T(8,128)} %refs_1_.2) | copy-start | bytes 196612
  15.6 5.8 %copy-start.3 = (f32[1,1,128,128]{3,2,1,0:T(8,128)S(1)}, f32[1,1,128,128]{3,2,1,0:T(8,128)}, u32[]{:S(2)}) copy-start(f32[1,1,128,128]{3,2,1,0:T(8,128)} %refs_3_.2) | copy-start | bytes 196612
  15.6 2.7 %collective-permute-start.8 = (f32[2,2,16,512]{3,2,1,0:T(8,128)S(1)}, f32[2,2,16,512]{3,2,1,0:T(8,128)S(1)}, u32[]{:S(2)}, u32[]{:S(2)}) collective-permute-start(f32[2,2,16,512]{3,2,1,0:T(8,128)S(1)} %shard_map.95), channel_id=1, source_target_pairs={{0,1},{1,0},{2,3},{3,2},{4,5},{5,4},{6,7},{7,6},{8,9},{9,8},{10,11... | collective-permute-start | bytes 393224 | tf_op jit(solution)/shard_map/ppermute | solution.py:181
  18.3 4.0 %collective-permute-start.9 = (f32[2,2,16,512]{3,2,1,0:T(8,128)S(1)}, f32[2,2,16,512]{3,2,1,0:T(8,128)S(1)}, u32[]{:S(2)}, u32[]{:S(2)}) collective-permute-start(f32[2,2,16,512]{3,2,1,0:T(8,128)S(1)} %shard_map.96), channel_id=1, source_target_pairs={{0,1},{1,0},{2,3},{3,2},{4,5},{5,4},{6,7},{7,6},{8,9},{9,8},{10,11... | collective-permute-start | bytes 393224 | tf_op jit(solution)/shard_map/ppermute | solution.py:181
